TPU v7x, 32 devices: a whole 2x2x4 slice. The times are simulated.
32 devices in a mesh: dp: 8 (over y, x, core), expert: 4 (over z).
Axes of the slice: x: 2, y: 2, z: 4, core: 2. Of those that a mesh axis runs over, the one named last changes fastest.
Arguments:
- tokens: bfloat16 [2, 8, 512, 1024], P(None, 'dp', 'expert'), may hold values from -6 to 6
- lengths: int32 [2, 8], P(None, 'dp'), may hold values from 128 to 512, as said below
- routes: int32 [2, 8, 512, 8], P(None, 'dp'), may hold values from 0 to 15, all different within a row; in each aligned block of 128 rows (0 to 127, 128 to 255, ..., all dimensions but the last counted through in order) at most 80 rows name the same one
- attn_gain: float32 [1024], replicated, may hold values from 0.5 to 1.5
- w_query: bfloat16 [1024, 1024], replicated, may hold values from -0.75 to 0.75
- w_keyval: bfloat16 [1024, 1024], replicated, may hold values from -0.75 to 0.75
- w_out: bfloat16 [1024, 1024], replicated, may hold values from -0.1875 to 0.1875
- ffn_gain: float32 [1024], replicated, may hold values from 0.5 to 1.5
- w_router: bfloat16 [1024, 16], replicated, may hold values from -0.09375 to 0.09375
- expert_gate_up: bfloat16 [16, 1024, 1024], P('expert'), may hold values from -0.1875 to 0.1875
- expert_down: bfloat16 [16, 512, 1024], P('expert'), may hold values from -1.5 to 1.5
- cotangent: bfloat16 [2, 8, 512, 1024], P(None, 'dp', 'expert'), may hold values from -6 to 6
Outputs:
- output: bfloat16 [2, 8, 512, 1024], P(None, 'dp', 'expert')
- input_grad: float32 [2, 8, 512, 1024], P(None, 'dp', 'expert')
- grad_attn_gain: float32 [1024], P(('dp', 'expert'))
- grad_query: float32 [1024, 1024], P(('dp', 'expert'))
- grad_keyval: float32 [1024, 1024], P(('dp', 'expert'))
- grad_out: float32 [1024, 1024], P(('dp', 'expert'))
- grad_ffn_gain: float32 [1024], P(('dp', 'expert'))
- grad_router: float32 [1024, 16], P(('dp', 'expert'))
- grad_gate_up: float32 [16, 1024, 1024], P('expert', 'dp')
- grad_down: float32 [16, 512, 1024], P('expert', 'dp')
Inputs may be any that keep to these rules, and one draw needn't show every extreme that they name: `lengths`: in every micro-batch one sequence has length 512; the others have 512 // 4 to 512. `routes`: each position names 8 different experts; in each aligned block of 128 positions (the positions of one device) no expert is named more than 80 times.
All inputs are finite; a program needn't handle non-finite values.
Results may differ from a plain program's by a relative error of at most 0.017.
The roundings to bfloat16 on the way count: a program that leaves them out, or rounds other values in their place, can miss the bound.
Values may be sent and summed in bfloat16 or wider, within the bound.
A program may use at most 192 MiB of HBM per device.

v0:
```python
import math

import jax
import jax.numpy as jnp
from jax import lax
from jax.sharding import PartitionSpec as P

HEAD_DIM = 64
CAP = 80


EPS = 1e-06
ATTENTION_SCALE = 0.015625
ROPE_BASE = 10000.0
NEG_FILL = -1e30


def rope_tables(positions, head_dim):
    half_dim = head_dim // 2
    frequency = jnp.exp(
        jnp.arange(half_dim, dtype=jnp.float32) * (-2.0 * math.log(ROPE_BASE) / head_dim)
    )
    angles = positions.astype(jnp.float32)[:, None] * frequency[None, :]
    return (jnp.cos(angles)[:, None, :], jnp.sin(angles)[:, None, :])


def rotate(operand, cos_table, sine_table):
    half_dim = operand.shape[-1] // 2
    front_half = operand[..., :half_dim]
    back_half = operand[..., half_dim:]
    return jnp.concatenate(
        [
            front_half * cos_table - back_half * sine_table,
            back_half * cos_table + front_half * sine_table,
        ],
        -1,
    )


def rms_scale(inputs):
    return lax.rsqrt(jnp.mean(inputs * inputs, -1, keepdims=True) + EPS)


def norm_backward(grad_normed, inputs, scale_rows, gain_vec):
    scaled = grad_normed * gain_vec
    gain_grad = jnp.sum(grad_normed * inputs * scale_rows, 0)
    input_part = scale_rows * (
        scaled - inputs * scale_rows * scale_rows * jnp.mean(scaled * inputs, -1, keepdims=True)
    )
    return (input_part, gain_grad)


def score_block(grouped_queries, partial_keys, query_pos, key_pos, seq_length):
    raw_scores = (
        jnp.einsum(
            "jclb,vcb->cljv", grouped_queries, partial_keys, preferred_element_type=jnp.float32
        )
        * ATTENTION_SCALE
    )
    allowed = (key_pos[None, :] <= query_pos[:, None]) & (key_pos[None, :] < seq_length)
    return jnp.where(allowed, raw_scores, NEG_FILL)


def slot_table(route_ids, is_live, experts, capacity, blocks):
    seq_len = route_ids.shape[0]
    block_rows = seq_len // blocks
    expert_ids = jnp.arange(experts, dtype=jnp.int32)
    named_hits = jnp.sum((route_ids[:, :, None] == expert_ids).astype(jnp.int32), 1) * is_live[
        :, None
    ].astype(jnp.int32)
    named_hits = named_hits.reshape(blocks, block_rows, experts)
    slot_rank = jnp.cumsum(named_hits, 1) - 1
    target = jnp.where(named_hits > 0, slot_rank, capacity)
    block_ids = jnp.broadcast_to(jnp.arange(blocks, dtype=jnp.int32)[:, None, None], target.shape)
    expert_grid = jnp.broadcast_to(expert_ids[None, None, :], target.shape)
    token_ids = jnp.broadcast_to(
        jnp.arange(block_rows, dtype=jnp.int32)[None, :, None], target.shape
    )
    block_table = jnp.full((blocks, experts, capacity + 1), block_rows, jnp.int32)
    block_table = block_table.at[block_ids, expert_grid, target].set(token_ids)
    return block_table[:, :, :capacity]


def expert_forward(received, route_table, filled, expert_base, w_router, w_gate_up, w_down):
    ff_width = w_down.shape[1]
    local_count = w_gate_up.shape[0]
    logits = jnp.einsum("sjcd,de->sjce", received, w_router, preferred_element_type=jnp.float32)
    chosen = jnp.take_along_axis(logits, route_table, axis=-1)
    weights = jax.nn.softmax(chosen, axis=-1)
    owned_ids = expert_base + jnp.arange(local_count, dtype=jnp.int32)
    gate_value = (
        jnp.sum(weights * (route_table == owned_ids[None, :, None, None]).astype(jnp.float32), -1)
        * filled
    )
    projected = jnp.einsum(
        "sjcd,jdf->sjcf", received, w_gate_up, preferred_element_type=jnp.float32
    )
    product = jax.nn.silu(projected[..., :ff_width]) * projected[..., ff_width:]
    activated = (product * gate_value[..., None]).astype(jnp.bfloat16)
    expert_out = jnp.einsum("sjcf,jfd->sjcd", activated, w_down, preferred_element_type=jnp.float32)
    return (expert_out, (projected, product, gate_value, activated))


def expert_backward(received, grad_rows, kept_state, w_gate_up, w_down):
    projected, product, gate_value, activated = kept_state
    ff_width = w_down.shape[1]
    grad_down = jnp.einsum(
        "sjcf,sjcd->jfd", activated, grad_rows, preferred_element_type=jnp.float32
    )
    grad_act = jnp.einsum("sjcd,jfd->sjcf", grad_rows, w_down, preferred_element_type=jnp.float32)
    grad_gate = jnp.sum(grad_act * product, -1)
    grad_product = grad_act * gate_value[..., None]
    gate_part = projected[..., :ff_width]
    up_part = projected[..., ff_width:]
    sigmoid_g = jax.nn.sigmoid(gate_part)
    grad_proj = jnp.concatenate(
        [
            grad_product * up_part * sigmoid_g * (1.0 + gate_part * (1.0 - sigmoid_g)),
            grad_product * gate_part * sigmoid_g,
        ],
        -1,
    ).astype(jnp.bfloat16)
    grad_gate_up = jnp.einsum(
        "sjcd,sjcf->jdf", received, grad_proj, preferred_element_type=jnp.float32
    )
    grad_inputs = jnp.einsum(
        "sjcf,jdf->sjcd", grad_proj, w_gate_up, preferred_element_type=jnp.float32
    )
    return (grad_inputs, grad_gate, grad_gate_up, grad_down)


def on_device(
    tokens,
    lengths,
    routes,
    attn_gain,
    w_query,
    w_keyval,
    w_out,
    ffn_gain,
    w_router,
    expert_gate_up,
    expert_down,
    cotangent,
):
    micro_count = tokens.shape[0]
    local_rows = tokens.shape[2]
    model_width = tokens.shape[3]
    owners = lax.axis_size("expert")
    my_index = lax.axis_index("expert")
    local_experts = expert_gate_up.shape[0]
    experts = w_router.shape[1]
    top_count = routes.shape[3]
    seq_len = routes.shape[2]
    head_dim = HEAD_DIM
    kv_width = w_keyval.shape[1] // 2
    kv_heads = kv_width // head_dim
    query_heads = w_query.shape[1] // head_dim
    group_size = query_heads // kv_heads
    capacity = CAP
    row_start = my_index * local_rows
    local_pos = row_start + jnp.arange(local_rows, dtype=jnp.int32)
    all_pos = jnp.arange(seq_len, dtype=jnp.int32)
    cos_local, sine_local = rope_tables(local_pos, head_dim)
    expert_base = my_index * local_experts
    expert_range = jnp.arange(experts, dtype=jnp.int32)
    zero_row = jnp.zeros((1, model_width), jnp.bfloat16)
    grad_attn_gain = jnp.zeros(attn_gain.shape, jnp.float32)
    grad_query = jnp.zeros(w_query.shape, jnp.float32)
    grad_keyval = jnp.zeros(w_keyval.shape, jnp.float32)
    grad_out_w = jnp.zeros(w_out.shape, jnp.float32)
    grad_ffn_gain = jnp.zeros(ffn_gain.shape, jnp.float32)
    grad_router = jnp.zeros(w_router.shape, jnp.float32)
    grad_gate_up = jnp.zeros(expert_gate_up.shape, jnp.float32)
    grad_down = jnp.zeros(expert_down.shape, jnp.float32)
    outputs = []
    input_grads = []
    for micro_index in range(micro_count):
        x_rows = tokens[micro_index, 0].astype(jnp.float32)
        seq_length = lengths[micro_index, 0]
        route_ids = routes[micro_index, 0]
        is_live_all = all_pos < seq_length
        keep_mask = (local_pos < seq_length).astype(jnp.float32)[:, None]
        scale_one = rms_scale(x_rows)
        normed = (x_rows * scale_one * attn_gain).astype(jnp.bfloat16)
        query_pre = jnp.dot(normed, w_query, preferred_element_type=jnp.float32)
        keyval_pre = jnp.dot(normed, w_keyval, preferred_element_type=jnp.float32)
        queries = rotate(
            query_pre.reshape(local_rows, query_heads, head_dim), cos_local, sine_local
        ).astype(jnp.bfloat16)
        rotary_keys = rotate(
            keyval_pre[:, :kv_width].reshape(local_rows, kv_heads, head_dim), cos_local, sine_local
        )
        keyval_local = jnp.concatenate(
            [rotary_keys.reshape(local_rows, kv_width), keyval_pre[:, kv_width:]], 1
        ).astype(jnp.bfloat16)
        keyval_all = lax.all_gather(keyval_local, "expert", axis=0, tiled=True)
        every_key_row = keyval_all[:, :kv_width].reshape(seq_len, kv_heads, head_dim)
        every_value_row = keyval_all[:, kv_width:].reshape(seq_len, kv_heads, head_dim)
        grouped_queries = queries.reshape(local_rows, kv_heads, group_size, head_dim)
        score_matrix = score_block(grouped_queries, every_key_row, local_pos, all_pos, seq_length)
        row_max = jnp.max(score_matrix, -1, keepdims=True)
        exp_scores = jnp.exp(score_matrix - row_max)
        row_total = jnp.sum(exp_scores, -1, keepdims=True)
        log_total = row_max + jnp.log(row_total)
        attention_probs = (exp_scores / row_total).astype(jnp.bfloat16)
        attention_mixture = jnp.einsum(
            "apzm,mau->zapu", attention_probs, every_value_row, preferred_element_type=jnp.float32
        )
        attention_mixture = attention_mixture.reshape(local_rows, query_heads * head_dim).astype(
            jnp.bfloat16
        )
        attn_out = jnp.dot(attention_mixture, w_out, preferred_element_type=jnp.float32)
        hidden = x_rows + keep_mask * attn_out
        scale_two = rms_scale(hidden)
        normed2 = (hidden * scale_two * ffn_gain).astype(jnp.bfloat16)
        block_table = slot_table(route_ids, is_live_all, experts, capacity, owners)
        my_table = lax.dynamic_index_in_dim(block_table, my_index, 0, keepdims=False)
        owned_table = lax.dynamic_slice_in_dim(block_table, expert_base, local_experts, 1)
        source_base = (jnp.arange(owners, dtype=jnp.int32) * local_rows)[:, None, None]
        is_filled = owned_table < local_rows
        global_table = jnp.where(is_filled, owned_table + source_base, seq_len)
        filled = is_filled.astype(jnp.float32)
        routes_padded = jnp.concatenate([route_ids, jnp.zeros((1, top_count), jnp.int32)], 0)
        route_table = routes_padded[global_table]
        flat_slots = my_table.reshape(-1)
        outgoing = jnp.concatenate([normed2, zero_row], 0)[my_table].reshape(
            owners, local_experts, capacity, model_width
        )
        received = lax.all_to_all(outgoing, "expert", split_axis=0, concat_axis=0, tiled=True)
        expert_out, kept_state = expert_forward(
            received, route_table, filled, expert_base, w_router, expert_gate_up, expert_down
        )
        returned = lax.all_to_all(
            expert_out.astype(jnp.bfloat16), "expert", split_axis=0, concat_axis=0, tiled=True
        ).astype(expert_out.dtype)
        expert_sum = (
            jnp.zeros((local_rows + 1, model_width), jnp.float32)
            .at[flat_slots]
            .add(returned.reshape(-1, model_width))[:local_rows]
        )
        outputs.append((hidden + expert_sum).astype(jnp.bfloat16))
        cot_rows = cotangent[micro_index, 0]
        outgoing_grad = jnp.concatenate([cot_rows, zero_row], 0)[my_table].reshape(
            owners, local_experts, capacity, model_width
        )
        grad_rows = lax.all_to_all(outgoing_grad, "expert", split_axis=0, concat_axis=0, tiled=True)
        grad_inputs, grad_gate, step_gate_up, step_down = expert_backward(
            received, grad_rows, kept_state, expert_gate_up, expert_down
        )
        grad_gate_up = grad_gate_up + step_gate_up
        grad_down = grad_down + step_down
        back_rows, back_gate = (
            lax.all_to_all(grad_inputs, "expert", split_axis=0, concat_axis=0, tiled=True),
            lax.all_to_all(grad_gate, "expert", split_axis=0, concat_axis=0, tiled=True),
        )
        slot_expert = jnp.repeat(expert_range, capacity)
        moe_grad = (
            jnp.zeros((local_rows + 1, model_width), jnp.float32)
            .at[flat_slots]
            .add(back_rows.reshape(-1, model_width))[:local_rows]
        )
        gate_grads = (
            jnp.zeros((local_rows + 1, experts), jnp.float32)
            .at[flat_slots, slot_expert]
            .add(back_gate.reshape(-1))[:local_rows]
        )
        local_routes = lax.dynamic_slice_in_dim(route_ids, row_start, local_rows, 0)
        logits = jnp.dot(normed2, w_router, preferred_element_type=jnp.float32)
        weights = jax.nn.softmax(jnp.take_along_axis(logits, local_routes, axis=1), axis=-1)
        chosen_grad = jnp.take_along_axis(gate_grads, local_routes, axis=1)
        chosen_grad = weights * (chosen_grad - jnp.sum(weights * chosen_grad, -1, keepdims=True))
        logit_grad = jnp.sum(
            chosen_grad[:, :, None]
            * (local_routes[:, :, None] == expert_range).astype(jnp.float32),
            1,
        ).astype(jnp.bfloat16)
        grad_router = grad_router + jnp.einsum(
            "td,te->de", normed2, logit_grad, preferred_element_type=jnp.float32
        )
        normed2_grad = moe_grad + jnp.einsum(
            "te,de->td", logit_grad, w_router, preferred_element_type=jnp.float32
        )
        hidden_part, gain_two = norm_backward(normed2_grad, hidden, scale_two, ffn_gain)
        grad_ffn_gain = grad_ffn_gain + gain_two
        hidden_grad = cot_rows.astype(jnp.float32) + hidden_part
        attn_grad = (hidden_grad * keep_mask).astype(jnp.bfloat16)
        grad_out_w = grad_out_w + jnp.einsum(
            "tq,td->qd", attention_mixture, attn_grad, preferred_element_type=jnp.float32
        )
        mix_grad = jnp.einsum(
            "td,qd->tq", attn_grad, w_out, preferred_element_type=jnp.float32
        ).astype(jnp.bfloat16)
        grouped_mixture = mix_grad.reshape(local_rows, kv_heads, group_size, head_dim)
        scores_again = score_block(grouped_queries, every_key_row, local_pos, all_pos, seq_length)
        prob_full = jnp.exp(scores_again - log_total)
        prob_grad = jnp.einsum(
            "jclb,vcb->cljv", grouped_mixture, every_value_row, preferred_element_type=jnp.float32
        )
        row_delta = jnp.sum(prob_full * prob_grad, -1, keepdims=True)
        score_gradient = (prob_full * (prob_grad - row_delta)).astype(jnp.bfloat16)
        prob_rounded = prob_full.astype(jnp.bfloat16)
        query_grad = (
            jnp.einsum(
                "apzm,mau->zapu", score_gradient, every_key_row, preferred_element_type=jnp.float32
            )
            * ATTENTION_SCALE
        )
        key_grad = (
            jnp.einsum(
                "vnxo,xvnc->ovc",
                score_gradient,
                grouped_queries,
                preferred_element_type=jnp.float32,
            )
            * ATTENTION_SCALE
        )
        value_grad = jnp.einsum(
            "vnxo,xvnc->ovc", prob_rounded, grouped_mixture, preferred_element_type=jnp.float32
        )
        keyval_grad = lax.psum_scatter(
            jnp.concatenate(
                [
                    key_grad.reshape(local_rows * lax.axis_size("expert"), kv_width),
                    value_grad.reshape(local_rows * lax.axis_size("expert"), kv_width),
                ],
                1,
            ).astype(jnp.bfloat16),
            "expert",
            scatter_dimension=0,
            tiled=True,
        ).astype(jnp.float32)
        key_back = rotate(
            keyval_grad[:, :kv_width].reshape(local_rows, kv_heads, head_dim),
            cos_local,
            -sine_local,
        )
        keyval_pre_grad = jnp.concatenate(
            [key_back.reshape(local_rows, kv_width), keyval_grad[:, kv_width:]], 1
        ).astype(jnp.bfloat16)
        query_back = rotate(
            query_grad.reshape(local_rows, query_heads, head_dim), cos_local, -sine_local
        )
        query_pre_grad = query_back.reshape(local_rows, query_heads * head_dim).astype(jnp.bfloat16)
        grad_query = grad_query + jnp.einsum(
            "td,tq->dq", normed, query_pre_grad, preferred_element_type=jnp.float32
        )
        grad_keyval = grad_keyval + jnp.einsum(
            "td,tk->dk", normed, keyval_pre_grad, preferred_element_type=jnp.float32
        )
        normed_grad = jnp.einsum(
            "tq,dq->td", query_pre_grad, w_query, preferred_element_type=jnp.float32
        )
        normed_grad = normed_grad + jnp.einsum(
            "tk,dk->td", keyval_pre_grad, w_keyval, preferred_element_type=jnp.float32
        )
        token_part, gain_one = norm_backward(normed_grad, x_rows, scale_one, attn_gain)
        grad_attn_gain = grad_attn_gain + gain_one
        input_grads.append(hidden_grad + token_part)
    dense_parts = (
        lax.psum_scatter(grad_attn_gain, ("dp", "expert"), scatter_dimension=0, tiled=True),
        lax.psum_scatter(grad_query, ("dp", "expert"), scatter_dimension=0, tiled=True),
        lax.psum_scatter(grad_keyval, ("dp", "expert"), scatter_dimension=0, tiled=True),
        lax.psum_scatter(grad_out_w, ("dp", "expert"), scatter_dimension=0, tiled=True),
        lax.psum_scatter(grad_ffn_gain, ("dp", "expert"), scatter_dimension=0, tiled=True),
        lax.psum_scatter(grad_router, ("dp", "expert"), scatter_dimension=0, tiled=True),
    )
    expert_parts = (
        lax.psum_scatter(
            grad_gate_up.astype(jnp.bfloat16), "dp", scatter_dimension=1, tiled=True
        ).astype(jnp.float32),
        lax.psum_scatter(
            grad_down.astype(jnp.bfloat16), "dp", scatter_dimension=1, tiled=True
        ).astype(jnp.float32),
    )
    output = jnp.stack(outputs)[:, None]
    input_grad = jnp.stack(input_grads)[:, None]
    return (
        output,
        input_grad,
        dense_parts[0],
        dense_parts[1],
        dense_parts[2],
        dense_parts[3],
        dense_parts[4],
        dense_parts[5],
        expert_parts[0],
        expert_parts[1],
    )


def solution(mesh):
    placed = (
        P(None, "dp", "expert", None),
        P(None, "dp"),
        P(None, "dp", None, None),
        P(),
        P(),
        P(),
        P(),
        P(),
        P(),
        P("expert", None, None),
        P("expert", None, None),
        P(None, "dp", "expert", None),
    )
    return jax.shard_map(
        on_device,
        mesh=mesh,
        in_specs=placed,
        out_specs=(
            P(None, "dp", "expert", None),
            P(None, "dp", "expert", None),
            P(("dp", "expert")),
            P(("dp", "expert"), None),
            P(("dp", "expert"), None),
            P(("dp", "expert"), None),
            P(("dp", "expert")),
            P(("dp", "expert"), None),
            P("expert", "dp", None),
            P("expert", "dp", None),
        ),
        check_vma=False,
    )
```

profile of v0, /device:TPU:0, one launch (start us, length us, event | category | flops | bytes accessed | tf_op | source)
XLA Modules:
  0.0 1736.7 jit_solution(6775757913261341340)
XLA Ops:
  45.9 30.8 %scatter_custom_fusion.4 = s32[5184]{0:T(1024)S(1)} fusion(s32[8192]{0:T(1024)S(1)} %reshape.882, s32[8192]{0:T(1024)S(1)} %reshape.884, s32[]{:T(128)} %constant.42.clone.1), kind=kCustom, calls=%fused_computation.311 | custom fusion | bytes 20740
  115.5 53.6 %all-to-all-done = bf16[4,4,80,1024]{3,2,1,0:T(8,128)(2,1)} async-done(((bf16[4,4,80,1024]{3,2,1,0:T(8,128)(2,1)}), bf16[4,4,80,1024]{3,2,1,0:T(8,128)(2,1)}, u32[]{:S(2)}, u32[]{:S(2)}) %all-to-all-start) | async-done | bytes 2621472 | tf_op jit(solution)/shard_map/all_to_all | solution.py:230
  174.3 31.2 %scatter_custom_fusion.5 = s32[5184]{0:T(1024)S(1)} fusion(s32[8192]{0:T(1024)S(1)} %reshape.888, s32[8192]{0:T(1024)} %copy-done.100, s32[]{:T(128)} %constant.42.clone.1), kind=kCustom, calls=%fused_computation.309 | custom fusion | bytes 21248
  214.2 98.2 %gather_fusion.6 = f32[10240]{0:T(1024)S(1)} fusion(f32[4,4,80,16]{2,3,1,0:T(8,128)S(1)} %fusion.177, s32[10240]{0:T(1024)S(1)} %reshape.949), kind=kCustom, calls=%fused_computation.clone | custom fusion | bytes 245760 | tf_op jit(solution)/shard_map/jit(take_along_axis)/gather | solution.py:88
  362.6 120.3 %all-to-all-done.5 = f32[4,4,80,1024]{3,2,1,0:T(8,128)} async-done(((f32[4,4,80,1024]{3,2,1,0:T(8,128)}), f32[4,4,80,1024]{3,2,1,0:T(8,128)}, u32[]{:S(2)}, u32[]{:S(2)}) %all-to-all-start.5) | async-done | bytes 5242912 | tf_op jit(solution)/shard_map/all_to_all | solution.py:254
  506.9 9.5 scatter_custom_fusion.6
  523.8 15.4 scatter_custom_fusion.2
  559.5 52.1 %all-to-all-done.2 = bf16[4,4,80,1024]{3,2,1,0:T(8,128)(2,1)} async-done(((bf16[4,4,80,1024]{3,2,1,0:T(8,128)(2,1)}), bf16[4,4,80,1024]{3,2,1,0:T(8,128)(2,1)}, u32[]{:S(2)}, u32[]{:S(2)}) %all-to-all-start.2) | async-done | bytes 2621472 | tf_op jit(solution)/shard_map/all_to_all | solution.py:230
  622.9 98.2 %gather_fusion.7 = f32[10240]{0:T(1024)S(1)} fusion(f32[4,4,80,16]{2,3,1,0:T(8,128)S(1)} %fusion.175, s32[10240]{0:T(1024)S(1)} %reshape.954), kind=kCustom, calls=%fused_computation.2.clone | custom fusion | bytes 245760 | tf_op jit(solution)/shard_map/jit(take_along_axis)/gather | solution.py:88
  760.7 49.1 %all-to-all-done.3 = bf16[4,4,80,1024]{3,2,1,0:T(8,128)(2,1)} async-done(((bf16[4,4,80,1024]{3,2,1,0:T(8,128)(2,1)}), bf16[4,4,80,1024]{3,2,1,0:T(8,128)(2,1)}, u32[]{:S(2)}, u32[]{:S(2)}) %all-to-all-start.3) | async-done | bytes 2621472 | tf_op jit(solution)/shard_map/all_to_all | solution.py:234
  815.7 14.7 scatter_custom_fusion
  854.7 14.9 scatter_custom_fusion.1
  869.6 60.4 %all-to-all-done.8 = f32[4,4,80,1024]{3,2,1,0:T(8,128)} async-done(((f32[4,4,80,1024]{3,2,1,0:T(8,128)}), f32[4,4,80,1024]{3,2,1,0:T(8,128)}, u32[]{:S(2)}, u32[]{:S(2)}) %all-to-all-start.8) | async-done | bytes 5242912 | tf_op jit(solution)/shard_map/all_to_all | solution.py:254
  930.0 15.4 scatter_custom_fusion.3
  987.6 9.5 fusion.5
  997.5 12.8 fusion.39
  1010.3 15.3 fusion.4
  1054.3 98.9 %reduce-scatter.29.cloned.1.call-done = f32[32,16]{1,0:T(8,128)} async-done(((f32[1024,16]{1,0:T(8,128)}), f32[32,16]{1,0:T(8,128)}) %reduce-scatter.29.cloned.1.call-update) | async-done | bytes 2064
  1154.5 49.8 %reduce-scatter.23.cloned.1.call-done = bf16[4,64,1024]{2,1,0:T(8,128)(2,1)} async-done(((bf16[4,512,1024]{2,1,0:T(8,128)(2,1)}), bf16[4,64,1024]{2,1,0:T(8,128)(2,1)}) %reduce-scatter.23.cloned.1.call-update) | async-done | bytes 524304 | tf_op jit(solution)/shard_map/reduce_scatter | solution.py:372
  1214.2 39.6 %all-reduce.8 = (f32[1024]{0:T(1024)S(1)}, f32[1024]{0:T(1024)S(1)}) all-reduce(f32[1024]{0:T(1024)S(1)} %add.421, f32[1024]{0:T(1024)S(1)} %copy-done.114), channel_id=4, replica_groups=mesh['dp'=8,'expert'=4] {'dp','expert'}, use_global_device_ids=true, to_apply=%region_46.49.clone | all-reduce | flops 2048 | bytes 16384
  1257.8 21.9 %reduce-scatter.21.cloned.1.call-done = bf16[4,128,1024]{2,1,0:T(8,128)(2,1)} async-done(((bf16[4,1024,1024]{2,1,0:T(8,128)(2,1)}), bf16[4,128,1024]{2,1,0:T(8,128)(2,1)}) %reduce-scatter.21.cloned.1.call-update) | async-done | bytes 1048592 | tf_op jit(solution)/shard_map/reduce_scatter | solution.py:369
  1282.6 148.2 %reduce-scatter.19.cloned.1.call-done = f32[32,1024]{1,0:T(8,128)} async-done(((f32[1024,1024]{1,0:T(8,128)}), f32[32,1024]{1,0:T(8,128)}) %reduce-scatter.19.cloned.1.call-update) | async-done | bytes 131088 | tf_op jit(solution)/shard_map/reduce_scatter | solution.py:364
  1430.8 149.5 %reduce-scatter.15.cloned.1.call-done = f32[32,1024]{1,0:T(8,128)} async-done(((f32[1024,1024]{1,0:T(8,128)}), f32[32,1024]{1,0:T(8,128)}) %reduce-scatter.15.cloned.1.call-update) | async-done | bytes 131088 | tf_op jit(solution)/shard_map/reduce_scatter | solution.py:362
  1580.3 149.3 %reduce-scatter.17.cloned.1.call-done = f32[32,1024]{1,0:T(8,128)} async-done(((f32[1024,1024]{1,0:T(8,128)}), f32[32,1024]{1,0:T(8,128)}) %reduce-scatter.17.cloned.1.call-update) | async-done | bytes 131088 | tf_op jit(solution)/shard_map/reduce_scatter | solution.py:363
  (566 shorter events, 361.4 us)
Async XLA Ops:
  7.2 78.5 %all-gather.3.cloned.1.call-start = ((), (), s32[]{:S(2)}) async-start(), calls=%async_computation.18 | async-start | bytes 1310720 | tf_op jit(solution)/shard_map/all_gather | solution.py:197
  103.0 66.1 %all-to-all-start = ((bf16[4,4,80,1024]{3,2,1,0:T(8,128)(2,1)}), bf16[4,4,80,1024]{3,2,1,0:T(8,128)(2,1)}, u32[]{:S(2)}, u32[]{:S(2)}) async-start(bf16[4,4,80,1024]{3,2,1,0:T(8,128)(2,1)} %bitcast.474), calls=%async_computation | async-start | bytes 5242880 | tf_op jit(solution)/shard_map/all_to_all | solution.py:230
  169.1 153.4 %all-to-all-start.4 = ((bf16[4,4,80,1024]{3,2,1,0:T(8,128)(2,1)}), bf16[4,4,80,1024]{3,2,1,0:T(8,128)(2,1)}, u32[]{:S(2)}, u32[]{:S(2)}) async-start(bf16[4,4,80,1024]{3,2,1,0:T(8,128)(2,1)} %bitcast.472), calls=%async_computation.4 | async-start | bytes 5242880 | tf_op jit(solution)/shard_map/all_to_all | solution.py:247
  214.2 98.9 %copy-start.121 = (pred[4,4,80]{2,1,0:T(4,128)(4,1)S(1)}, pred[4,4,80]{2,1,0:T(4,128)(4,1)}, u32[]{:S(2)}) copy-start(pred[4,4,80]{2,1,0:T(4,128)(4,1)} %get-tuple-element.123) | copy-start | bytes 3844
  313.1 240.0 %copy-start.87 = (f32[4,4,80]{2,0,1:T(4,128)}, f32[4,4,80]{2,0,1:T(4,128)S(1)}, u32[]{:S(2)}) copy-start(f32[4,4,80]{2,0,1:T(4,128)S(1)} %copy.381) | copy-start | bytes 15364
  332.4 13.8 all-to-all-start.6
  346.2 136.7 %all-to-all-start.5 = ((f32[4,4,80,1024]{3,2,1,0:T(8,128)}), f32[4,4,80,1024]{3,2,1,0:T(8,128)}, u32[]{:S(2)}, u32[]{:S(2)}) async-start(f32[4,4,80,1024]{3,2,1,0:T(8,128)} %copy.409), calls=%async_computation.5 | async-start | bytes 10485760 | tf_op jit(solution)/shard_map/all_to_all | solution.py:254
  351.5 138.5 %all-gather.5.cloned.1.call-start = ((), (), s32[]{:S(2)}) async-start(), calls=%async_computation.19 | async-start | bytes 1310720 | tf_op jit(solution)/shard_map/all_gather | solution.py:197
  482.9 65.0 %all-to-all-start.7 = ((bf16[4,4,80,1024]{3,2,1,0:T(8,128)(2,1)}), bf16[4,4,80,1024]{3,2,1,0:T(8,128)(2,1)}, u32[]{:S(2)}, u32[]{:S(2)}) async-start(bf16[4,4,80,1024]{3,2,1,0:T(8,128)(2,1)} %bitcast.471), calls=%async_computation.7 | async-start | bytes 5242880 | tf_op jit(solution)/shard_map/all_to_all | solution.py:247
  547.9 63.8 %all-to-all-start.2 = ((bf16[4,4,80,1024]{3,2,1,0:T(8,128)(2,1)}), bf16[4,4,80,1024]{3,2,1,0:T(8,128)(2,1)}, u32[]{:S(2)}, u32[]{:S(2)}) async-start(bf16[4,4,80,1024]{3,2,1,0:T(8,128)(2,1)} %bitcast.473), calls=%async_computation.2 | async-start | bytes 5242880 | tf_op jit(solution)/shard_map/all_to_all | solution.py:230
  611.6 123.8 %all-to-all-start.1 = ((bf16[4,4,80,1024]{3,2,1,0:T(8,128)(2,1)}), bf16[4,4,80,1024]{3,2,1,0:T(8,128)(2,1)}, u32[]{:S(2)}, u32[]{:S(2)}) async-start(bf16[4,4,80,1024]{3,2,1,0:T(8,128)(2,1)} %copy.382), calls=%async_computation.1 | async-start | bytes 5242880 | tf_op jit(solution)/shard_map/all_to_all | solution.py:234
  735.4 11.4 all-to-all-start.9
  746.8 63.0 %all-to-all-start.3 = ((bf16[4,4,80,1024]{3,2,1,0:T(8,128)(2,1)}), bf16[4,4,80,1024]{3,2,1,0:T(8,128)(2,1)}, u32[]{:S(2)}, u32[]{:S(2)}) async-start(bf16[4,4,80,1024]{3,2,1,0:T(8,128)(2,1)} %copy.407), calls=%async_computation.3 | async-start | bytes 5242880 | tf_op jit(solution)/shard_map/all_to_all | solution.py:234
  809.8 120.2 %all-to-all-start.8 = ((f32[4,4,80,1024]{3,2,1,0:T(8,128)}), f32[4,4,80,1024]{3,2,1,0:T(8,128)}, u32[]{:S(2)}, u32[]{:S(2)}) async-start(f32[4,4,80,1024]{3,2,1,0:T(8,128)} %copy.421), calls=%async_computation.8 | async-start | bytes 10485760 | tf_op jit(solution)/shard_map/all_to_all | solution.py:254
  814.9 223.6 %reduce-scatter.25.cloned.1.call-start = ((), (), s32[]{:S(2)}) async-start(), calls=%async_computation.25 | async-start | bytes 1310720
  962.6 81.0 %reduce-scatter.27.cloned.1.call-start = ((), (), s32[]{:S(2)}) async-start(), calls=%async_computation.26 | async-start | bytes 1310720
  977.8 175.4 %reduce-scatter.29.cloned.1.call-start = ((), (), s32[]{:S(2)}) async-start(), calls=%async_computation.27 | async-start | bytes 540672
  987.5 216.8 %reduce-scatter.23.cloned.1.call-start = ((), (), s32[]{:S(2)}) async-start(), calls=%async_computation.24 | async-start | bytes 4718592 | tf_op jit(solution)/shard_map/reduce_scatter | solution.py:372
  997.1 282.7 %reduce-scatter.21.cloned.1.call-start = ((), (), s32[]{:S(2)}) async-start(), calls=%async_computation.23 | async-start | bytes 9437184 | tf_op jit(solution)/shard_map/reduce_scatter | solution.py:369
  1025.7 405.1 %reduce-scatter.19.cloned.1.call-start = ((), (), s32[]{:S(2)}) async-start(), calls=%async_computation.22 | async-start | bytes 4325376 | tf_op jit(solution)/shard_map/reduce_scatter | solution.py:364
  1030.3 550.0 %reduce-scatter.15.cloned.1.call-start = ((), (), s32[]{:S(2)}) async-start(), calls=%async_computation.20 | async-start | bytes 4325376 | tf_op jit(solution)/shard_map/reduce_scatter | solution.py:362
  1038.4 691.2 %reduce-scatter.17.cloned.1.call-start = ((), (), s32[]{:S(2)}) async-start(), calls=%async_computation.21 | async-start | bytes 4325376 | tf_op jit(solution)/shard_map/reduce_scatter | solution.py:363
  1054.3 152.3 %copy-start.112 = (f32[1024]{0:T(1024)S(1)}, f32[1024]{0:T(1024)}, u32[]{:S(2)}) copy-start(f32[1024]{0:T(1024)} %get-tuple-element.94) | copy-start | bytes 12292
  1054.3 152.3 %copy-start.113 = (f32[1024]{0:T(1024)S(1)}, f32[1024]{0:T(1024)}, u32[]{:S(2)}) copy-start(f32[1024]{0:T(1024)} %get-tuple-element.92) | copy-start | bytes 12292
  (133 other events, 2204.4 us)
Sparse Core Ops, SparseCore 0:
  16.0 30.6 all-gather.2
  354.4 53.9 all-gather.4
  962.7 26.2 reduce-scatter.24
  991.9 25.7 reduce-scatter.26
  1020.4 132.7 reduce-scatter.28
  1156.7 47.5 reduce-scatter.22
  1207.8 71.9 reduce-scatter.20
  1282.7 148.0 reduce-scatter.18
  1433.7 146.5 reduce-scatter.14
  1583.1 146.4 reduce-scatter.16
where the time goes:
time: 1740 us
  waiting for transfers between devices  953 us (55%)
  local copies, waits for them, and re-layouts  392 us (23%)
  matrix products  152 us (9%)
  other arithmetic  130 us (7%)
  starting transfers between devices  53.1 us (3%)
  blocking collectives  39.6 us (2%)
    gather x10, local copies, waits for them, and re-layouts, expert_forward(): chosen = jnp.take_along_axis(logits, route_table, axis=-1)  199 us
    all_to_all x2, waiting for transfers between devices, on_device(): lax.all_to_all(grad_inputs, 'expert', split_axis=0, concat_axis=0, tiled=...  181 us
    reduce_scatter x1, waiting for transfers between devices, on_device(): lax.psum_scatter(grad_query, ('dp', 'expert'), scatter_dimension=0, tiled...  150 us
    reduce_scatter x1, waiting for transfers between devices, on_device(): lax.psum_scatter(grad_keyval, ('dp', 'expert'), scatter_dimension=0, tile...  149 us
    reduce_scatter x1, waiting for transfers between devices, on_device(): lax.psum_scatter(grad_out_w, ('dp', 'expert'), scatter_dimension=0, tiled...  148 us
    all_to_all x2, waiting for transfers between devices, on_device(): lax.all_to_all(outgoing, 'expert', split_axis=0, concat_axis=0, tiled=True)  106 us
    unnamed x13, waiting for transfers between devices  99 us
    unnamed x295, local copies, waits for them, and re-layouts  93.6 us
  transfers between devices with their start and end apart: 20, of which 11 were waited for; matrix products, arithmetic and copies ran while one was open for 34% of the time, Pallas kernels for 0%

commit v1 on v0

v1 whole, which is shorter than its diff:
```python
import functools
import math

import jax
import jax.numpy as jnp
import numpy as np
from jax import lax
from jax.experimental import pallas as pl
from jax.experimental.pallas import tpu as pltpu
from jax.sharding import PartitionSpec as P

HEAD_DIM = 64
EPS = 1e-06
ATTENTION_SCALE = 0.015625
ROPE_BASE = 10000.0
NEG_FILL = -1e30
LANES = 128
STRIP = 16
BF = jnp.bfloat16
F32 = jnp.float32
VMEM_LIMIT = 62 * 2**20


def dot_of(left, right, left_dim, right_dim):
    return lax.dot_general(
        left, right, (((left_dim,), (right_dim,)), ((), ())), preferred_element_type=F32
    )


def nn(left, right):
    return dot_of(left, right, 1, 0)


def nt(left, right):
    return dot_of(left, right, 1, 1)


def tn(left, right):
    return dot_of(left, right, 0, 0)


def rope_constants(seq_len):
    half = HEAD_DIM // 2
    frequency = np.exp(
        np.arange(half, dtype=np.float32) * np.float32(-2.0 * math.log(ROPE_BASE) / HEAD_DIM)
    ).astype(np.float32)
    angles = np.arange(seq_len, dtype=np.float32)[:, None] * frequency[None, :]
    cos, sin = np.cos(angles).astype(np.float32), np.sin(angles).astype(np.float32)
    heads = LANES // HEAD_DIM
    return np.tile(np.concatenate([cos, cos], 1), (1, heads)), np.tile(
        np.concatenate([-sin, sin], 1), (1, heads)
    )


def lane_ids(rows):
    return lax.broadcasted_iota(jnp.int32, (rows, LANES), 1)


def swap_halves(chunk):
    half = HEAD_DIM // 2
    first = lax.rem(lane_ids(chunk.shape[0]), HEAD_DIM) < half
    return jnp.where(
        first, pltpu.roll(chunk, LANES - half, 1), pltpu.roll(chunk, half, 1)
    )


def rope(chunk, cos, sin):
    return chunk * cos + swap_halves(chunk) * sin


def rms_scale(rows):
    return lax.rsqrt(jnp.mean(rows * rows, -1, keepdims=True) + EPS)


def stack_heads(first, second):
    low = lane_ids(first.shape[0]) < HEAD_DIM
    zero = jnp.zeros_like(first)
    return [
        jnp.where(low, first, zero),
        jnp.where(low, pltpu.roll(first, HEAD_DIM, 1), zero),
        jnp.where(low, zero, pltpu.roll(second, HEAD_DIM, 1)),
        jnp.where(low, zero, second),
    ]


def unstack_heads(stacked, rows):
    low = lane_ids(rows) < HEAD_DIM
    parts = [stacked[k * rows : (k + 1) * rows] for k in range(4)]
    first = jnp.where(low, parts[0], pltpu.roll(parts[1], HEAD_DIM, 1))
    second = jnp.where(low, pltpu.roll(parts[2], HEAD_DIM, 1), parts[3])
    return first, second


def rows_at(index, rows):
    return pl.ds(pl.multiple_of(index * rows, rows), rows)


class Gather:
    def __init__(self, buffer, micro, rows, count, sems, up=True, down=True):
        self.buffer, self.micro, self.rows, self.count, self.sems = buffer, micro, rows, count, sems
        self.ways = [w for w, on in ((0, up), (1, down)) if on]

    def copy(self, way, step, block):
        z = lax.axis_index("expert")
        target = z + 1 if way == 0 else z - 1
        view = self.buffer.at[self.micro, rows_at(block, self.rows), :]
        return pltpu.make_async_remote_copy(
            src_ref=view,
            dst_ref=view,
            send_sem=self.sems.at[0, way, step],
            recv_sem=self.sems.at[1, way, step],
            device_id={"expert": target},
            device_id_type=pl.DeviceIdType.MESH,
        )

    def sends(self, way, step):
        z = lax.axis_index("expert")
        if way == 0:
            return z - step, jnp.logical_and(z < self.count - 1, z - step >= 0)
        return z + step, jnp.logical_and(z > 0, z + step <= self.count - 1)

    def receives(self, way, step):
        z = lax.axis_index("expert")
        if way == 0:
            return z - 1 - step, z - 1 - step >= 0
        return z + 1 + step, z + 1 + step <= self.count - 1

    def start(self, step):
        for way in self.ways:
            block, on = self.sends(way, step)

            @pl.when(on)
            def _(way=way, block=block):
                self.copy(way, step, block).start()

    def wait(self, step):
        for way in self.ways:
            block, on = self.receives(way, step)

            @pl.when(on)
            def _(way=way, block=block):
                self.copy(way, step, block).wait_recv()

    def hop(self, step):
        self.wait(step)
        if step + 1 < self.count - 1:
            self.start(step + 1)

    def finish(self):
        for step in range(self.count - 1):
            for way in self.ways:
                block, on = self.sends(way, step)

                @pl.when(on)
                def _(way=way, step=step, block=block):
                    self.copy(way, step, block).wait_send()


class Reduce:
    def __init__(self, parts, landing, rows, count, sems, up=True, down=True):
        self.parts, self.landing = parts, landing
        self.rows, self.count, self.sems = rows, count, sems
        self.ways = [w for w, on in ((0, up), (1, down)) if on]

    def block(self, way, slot):
        z = lax.axis_index("expert")
        if way == 0:
            return z + self.count - 1 - slot, slot >= z
        return z - (self.count - 1) + slot, slot >= self.count - 1 - z

    def place(self, way, slot, z):
        if way == 0:
            return slot - (z - 1)
        return self.count - (slot - (self.count - 2 - z))

    def copy(self, way, slot, block):
        z = lax.axis_index("expert")
        target = z + 1 if way == 0 else z - 1
        return pltpu.make_async_remote_copy(
            src_ref=self.parts.at[rows_at(block, self.rows), :],
            dst_ref=self.landing.at[self.place(way, slot, target)],
            send_sem=self.sems.at[0, way, slot],
            recv_sem=self.sems.at[1, way, slot],
            device_id={"expert": target},
            device_id_type=pl.DeviceIdType.MESH,
        )

    def arrival(self, way, slot, block):
        z = lax.axis_index("expert")
        source = z - 1 if way == 0 else z + 1
        return pltpu.make_async_remote_copy(
            src_ref=self.parts.at[rows_at(block, self.rows), :],
            dst_ref=self.landing.at[self.place(way, slot, z)],
            send_sem=self.sems.at[0, way, slot],
            recv_sem=self.sems.at[1, way, slot],
            device_id={"expert": source},
            device_id_type=pl.DeviceIdType.MESH,
        )

    def inner(self, way):
        z = lax.axis_index("expert")
        return z >= 1 if way == 0 else z <= self.count - 2

    def slot(self, slot):
        z = lax.axis_index("expert")
        for way in self.ways:
            block, on = self.block(way, slot)
            if slot >= 1:

                @pl.when(jnp.logical_and(on, self.inner(way)))
                def _(way=way, block=block):
                    self.arrival(way, slot - 1, block).wait_recv()
                    if slot < self.count - 1:
                        where = rows_at(block, self.rows)
                        total = self.parts[where, :].astype(F32) + self.landing[
                            self.place(way, slot - 1, z)
                        ].astype(F32)
                        self.parts[where, :] = total.astype(self.parts.dtype)

            if slot < self.count - 1:

                @pl.when(on)
                def _(way=way, block=block):
                    self.copy(way, slot, block).start()

    def total(self, out):
        z = lax.axis_index("expert")
        out[...] = self.parts[rows_at(z, self.rows), :].astype(F32)
        for way in self.ways:

            @pl.when(self.inner(way))
            def _(way=way):
                out[...] += self.landing[self.place(way, self.count - 2, z)].astype(F32)

    def finish(self):
        for slot in range(self.count - 1):
            for way in self.ways:
                block, on = self.block(way, slot)

                @pl.when(on)
                def _(way=way, slot=slot, block=block):
                    self.copy(way, slot, block).wait_send()


def line_barrier(count):
    z = lax.axis_index("expert")
    barrier = pltpu.get_barrier_semaphore()
    for target, on in ((z + 1, z < count - 1), (z - 1, z > 0)):

        @pl.when(on)
        def _(target=target):
            pl.semaphore_signal(
                barrier, inc=1, device_id={"expert": target}, device_id_type=pl.DeviceIdType.MESH
            )

    pl.semaphore_wait(barrier, (z > 0).astype(jnp.int32) + (z < count - 1).astype(jnp.int32))


def masked_scores(scores_ref, strip, rows, seq_len, row_base, length):
    where = rows_at(strip, STRIP)
    shape = (STRIP, seq_len)
    first = row_base + lax.rem(strip * STRIP, rows)
    query_pos = first + lax.broadcasted_iota(jnp.int32, shape, 0)
    key_pos = lax.broadcasted_iota(jnp.int32, shape, 1)
    allowed = jnp.logical_and(key_pos <= query_pos, key_pos < length)
    return jnp.where(allowed, scores_ref[where, :] * ATTENTION_SCALE, NEG_FILL)


def softmax_rows(scores):
    top = jnp.max(scores, -1, keepdims=True)
    raised = jnp.exp(scores - top)
    return raised / jnp.sum(raised, -1, keepdims=True)


def forward_kernel(
    dims,
    lengths,
    tokens,
    cot,
    routes,
    gain_one,
    gain_two,
    cos_ref,
    sin_ref,
    router,
    query_hbm,
    keyval_hbm,
    out_hbm,
    gate_up_hbm,
    down_hbm,
    y_out,
    hidden_out,
    moe_out,
    queries_out,
    keyval_out,
    mixture_out,
    grad_gu_out,
    grad_dn_out,
    wide,
    narrow,
    normed,
    queries,
    keyval,
    mixture,
    hidden,
    named,
    gates,
    router_pad,
    rows_all,
    cot_all,
    acts,
    d_proj,
    w_out,
    w_gu,
    w_dn,
    out_parts,
    out_land,
    in_parts,
    in_land,
    own_sum,
    moe_sum,
    kv_sems,
    rows_sems,
    cot_sems,
    out_sems,
    in_sems,
    load_sems,
    store_sems,
):
    micros, rows, count, local, ff, model = dims
    seq_len = count * rows
    kv = keyval.shape[2] // 2
    chunks = kv // LANES
    z = lax.axis_index("expert")
    row_base = z * rows
    split = -(-model // seq_len)
    piece = model // split
    back = wide
    scores = wide.at[0 : 4 * rows, 0:seq_len]
    probs = d_proj.at[micros * local - 1, 0 : 4 * rows, 0:seq_len]
    tile = 512

    loads = []

    def load(src, dst):
        copy = pltpu.make_async_copy(src, dst, load_sems.at[len(loads)])
        copy.start()
        loads.append(copy)
        return copy

    early = []
    for index, weight in enumerate((query_hbm, keyval_hbm)):
        early.append(
            [
                load(
                    weight.at[pl.ds(k * piece, piece), :],
                    d_proj.at[index * split + k, pl.ds(0, piece), :],
                )
                for k in range(split)
            ]
        )
    load_out = load(out_hbm, w_out)
    load_gu = load(gate_up_hbm, w_gu)
    load_dn = load(down_hbm, w_dn)

    line_barrier(count)

    gather_kv = [
        Gather(keyval, m, rows, count, kv_sems.at[m], down=False) for m in range(micros)
    ]
    gather_rows = [Gather(rows_all, m, rows, count, rows_sems.at[m]) for m in range(micros)]
    gather_cot = [Gather(cot_all, m, rows, count, cot_sems.at[m]) for m in range(micros)]
    reduce_out = [
        Reduce(out_parts, out_land, rows, count, out_sems.at[m]) for m in range(micros)
    ]
    reduce_in = [Reduce(in_parts, in_land, rows, count, in_sems.at[m]) for m in range(micros)]

    for m in range(micros):
        cot_all[m, rows_at(z, rows), :] = cot[m, 0]
    gather_cot[0].start(0)

    for m in range(micros):
        x_rows = tokens[m, 0].astype(F32)
        normed[m * rows : (m + 1) * rows, :] = (
            x_rows * rms_scale(x_rows) * gain_one[...]
        ).astype(BF)
    cos = cos_ref[rows_at(z, rows), :]
    sin = sin_ref[rows_at(z, rows), :]
    both = micros * rows

    def project(index):
        for copy in early[index]:
            copy.wait()
        total = None
        for k in range(split):
            part = nn(
                normed[:, k * piece : (k + 1) * piece], d_proj[index * split + k, 0:piece, :]
            )
            total = part if total is None else total + part
        wide[0:both, :] = total

    project(1)
    for m in range(micros):
        span = slice(m * rows, (m + 1) * rows)
        for c in range(chunks):
            lanes = slice(c * LANES, (c + 1) * LANES)
            keyval[m, rows_at(z, rows), lanes] = rope(wide[span, lanes], cos, sin).astype(BF)
        keyval[m, rows_at(z, rows), kv:] = wide[span, kv:].astype(BF)
        gather_kv[m].start(0)
        for b in range(count):

            @pl.when(b > z)
            def _(m=m, b=b):
                keyval[m, b * rows : (b + 1) * rows, :] = jnp.zeros((rows, 2 * kv), BF)

    project(0)
    for m in range(micros):
        span = slice(m * rows, (m + 1) * rows)
        for i in range(chunks):
            pair = [
                rope(wide[span, c * LANES : (c + 1) * LANES], cos, sin)
                for c in (2 * i, 2 * i + 1)
            ]
            for k, block in enumerate(stack_heads(*pair)):
                queries[m, i, k * rows : (k + 1) * rows, :] = block.astype(BF)

    for m in range(micros):
        lane = lane_ids(seq_len)
        hit = jnp.zeros((seq_len, LANES), F32)
        for k in range(routes.shape[3]):
            hit = hit + (routes[m, 0][:, k : k + 1] == lane).astype(F32)
        live = lax.broadcasted_iota(jnp.int32, (seq_len, LANES), 0) < lengths[m, 0]
        named[m] = jnp.where(live, hit, 0.0)
    router_pad[...] = jnp.zeros(router_pad.shape, BF)
    router_pad[:, 0 : router.shape[1]] = router[...]

    def attend(m):
        length = lengths[m, 0]
        for i in range(chunks):
            lanes = slice(i * LANES, (i + 1) * LANES)
            scores[...] = nt(queries[m, i], keyval[m, :, lanes])

            def strip_step(strip, carry):
                probs[rows_at(strip, STRIP), :] = softmax_rows(
                    masked_scores(scores, strip, rows, seq_len, row_base, length)
                ).astype(BF)
                return carry

            lax.fori_loop(0, 4 * rows // STRIP, strip_step, 0)
            mixed = nn(probs[...], keyval[m, :, kv + i * LANES : kv + (i + 1) * LANES])
            first, second = unstack_heads(mixed, rows)
            mixture[m, :, 2 * i * LANES : (2 * i + 1) * LANES] = first.astype(BF)
            mixture[m, :, (2 * i + 1) * LANES : (2 * i + 2) * LANES] = second.astype(BF)
        if m == 0:
            load_out.wait()
        live = (row_base + lax.broadcasted_iota(jnp.int32, (rows, 1), 0)) < length
        rows_hidden = tokens[m, 0].astype(F32) + jnp.where(
            live, nn(mixture[m], w_out[...]), 0.0
        )
        hidden[m] = rows_hidden
        rows_all[m, rows_at(z, rows), :] = (
            rows_hidden * rms_scale(rows_hidden) * gain_two[...]
        ).astype(BF)
        gather_rows[m].start(0)

    def gate_rows(m):
        logits = nn(rows_all[m], router_pad[...])
        on = named[m] > 0.0
        masked = jnp.where(on, logits, NEG_FILL)
        raised = jnp.where(on, jnp.exp(masked - jnp.max(masked, -1, keepdims=True)), 0.0)
        total = jnp.sum(raised, -1, keepdims=True)
        gates[...] = raised / jnp.where(total > 0.0, total, 1.0)

    def column(block, expert):
        return jnp.sum(
            jnp.where(lane_ids(block.shape[0]) == expert, block, 0.0), -1, keepdims=True
        )

    def expert_forward(m, j):
        expert = z * local + j
        wide[...] = nn(rows_all[m], w_gu[j])

        def strip_step(strip, carry):
            where = rows_at(strip, STRIP)
            gate = column(gates[where, :], expert)
            front, up = wide[where, 0:ff], wide[where, ff:]
            silu = front / (1.0 + jnp.exp(-front))
            acts[m, where, j * ff : (j + 1) * ff] = (silu * up * gate).astype(BF)
            d_proj[m * local + j, where, :] = wide[where, :].astype(BF)
            return carry

        lax.fori_loop(0, seq_len // STRIP, strip_step, 0)

    def expert_backward(m, j):
        expert = z * local + j
        narrow[...] = nt(cot_all[m], w_dn[j * ff : (j + 1) * ff, :])

        def strip_step(strip, carry):
            where = rows_at(strip, STRIP)
            gate = column(gates[where, :], expert)
            front = d_proj[m * local + j, where, 0:ff].astype(F32)
            up = d_proj[m * local + j, where, ff:].astype(F32)
            d_act = narrow[where, :]
            sigmoid = 1.0 / (1.0 + jnp.exp(-front))
            silu = front * sigmoid
            d_gate = jnp.sum(d_act * silu * up, -1, keepdims=True)
            d_prod = d_act * gate
            d_proj[m * local + j, where, 0:ff] = (
                d_prod * up * sigmoid * (1.0 + front * (1.0 - sigmoid))
            ).astype(BF)
            d_proj[m * local + j, where, ff:] = (d_prod * silu).astype(BF)
            lane = lane_ids(STRIP)
            mine = jnp.where(lane == expert, d_gate, 0.0) * named[m, where, :]
            if j == 0:
                in_parts[where, model:] = mine.astype(BF)
            else:
                in_parts[where, model:] = (
                    in_parts[where, model:].astype(F32) + mine
                ).astype(BF)
            return carry

        lax.fori_loop(0, seq_len // STRIP, strip_step, 0)
        for r in range(0, seq_len, tile):
            span = slice(r, r + tile)
            part = nt(d_proj[m * local + j, span, :], w_gu[j])
            if j == 0:
                back[span, :] = part
            elif j < local - 1:
                back[span, :] += part
            else:
                in_parts[span, 0:model] = (back[span, :] + part).astype(BF)

    def weight_grads(j):
        for part_of in range(4):
            lanes = slice(part_of * ff // 2, (part_of + 1) * ff // 2)
            total = None
            for m in range(micros):
                part = tn(rows_all[m], d_proj[m * local + j, :, lanes])
                total = part if total is None else total + part
            w_gu[j, :, lanes] = total.astype(BF)
        total = None
        for m in range(micros):
            part = tn(acts[m, :, j * ff : (j + 1) * ff], cot_all[m])
            total = part if total is None else total + part
        w_dn[j * ff : (j + 1) * ff, :] = total.astype(BF)

    steps = count - 1

    def run(*todo):
        for item in todo:
            item()

    def hops(gather, first=0, last=steps):
        for step in range(first, last):
            gather.hop(step)

    gather_kv[0].hop(0)
    gather_cot[0].hop(0)
    hops(gather_kv[0], 1)
    gather_kv[1].hop(0)
    attend(0)
    hops(gather_cot[0], 1)
    hops(gather_kv[1], 1)
    gather_rows[0].hop(0)
    attend(1)
    gather_cot[1].start(0)
    hops(gather_rows[0], 1)
    gather_rows[1].hop(0)

    load_gu.wait()
    load_dn.wait()
    queue = []

    def advance(amount=1):
        for _ in range(amount):
            if queue:
                queue.pop(0)()

    def finish_out(m):
        reduce_out[m].total(own_sum)
        y_out[m, 0] = (hidden[m] + own_sum[...]).astype(BF)
        reduce_out[m].finish()

    def finish_in(m):
        reduce_in[m].total(moe_sum.at[m])
        reduce_in[m].finish()

    def slots(reduce):
        return [functools.partial(reduce.slot, t) for t in range(count)]

    queue += [functools.partial(gather_cot[1].hop, 0)]
    for step in range(1, steps):
        queue += [functools.partial(gather_rows[1].hop, step)]
        queue += [functools.partial(gather_cot[1].hop, step)]
    for m in range(micros):
        if m == 1:
            while queue:
                advance()
            queue += slots(reduce_in[0]) + [functools.partial(finish_in, 0)]
        gate_rows(m)
        for j in range(local):
            expert_forward(m, j)
            advance()
        while queue:
            advance()
        for r in range(0, seq_len, tile):
            out_parts[r : r + tile, :] = nn(acts[m, r : r + tile, :], w_dn[...]).astype(BF)
        queue += slots(reduce_out[m]) + [functools.partial(finish_out, m)]
        for j in range(local):
            expert_backward(m, j)
            advance()
    while queue:
        advance()
    queue += slots(reduce_in[1]) + [functools.partial(finish_in, 1)]
    stores = []

    def store(src, dst):
        copy = pltpu.make_async_copy(src, dst, store_sems.at[len(stores)])
        copy.start()
        stores.append(copy)

    advance()
    for j in range(local):
        weight_grads(j)
        advance()
        store(w_gu.at[j], grad_gu_out.at[j])
        store(w_dn.at[pl.ds(j * ff, ff), :], grad_dn_out.at[pl.ds(j * ff, ff), :])
    while queue:
        advance()
    store(hidden, hidden_out)
    store(moe_sum, moe_out)
    store(queries, queries_out)
    store(keyval, keyval_out)
    store(mixture, mixture_out)
    for item in gather_kv + gather_rows + gather_cot:
        item.finish()
    for copy in stores:
        copy.wait()


def forward_call(
    count, tokens, lengths, routes, gain_one, w_query, w_keyval, w_out, gain_two, w_router,
    gate_up, down, cot,
):
    micros, _, rows, model = tokens.shape
    local, ff = gate_up.shape[0], down.shape[1]
    seq_len = routes.shape[2]
    kv = w_keyval.shape[1] // 2
    chunks = kv // LANES
    heads = w_query.shape[1]
    steps = count - 1
    split = -(-model // seq_len)
    cos, sin = rope_constants(seq_len)
    vmem = pl.BlockSpec(memory_space=pltpu.VMEM)
    smem = pl.BlockSpec(memory_space=pltpu.SMEM)
    hbm = pl.BlockSpec(memory_space=pl.ANY)
    dma = pltpu.SemaphoreType.DMA
    wide_in = model + LANES
    out_shape = (
        jax.ShapeDtypeStruct((micros, 1, rows, model), BF),
        jax.ShapeDtypeStruct((micros, rows, model), F32),
        jax.ShapeDtypeStruct((micros, rows, wide_in), F32),
        jax.ShapeDtypeStruct((micros, chunks, 4 * rows, LANES), BF),
        jax.ShapeDtypeStruct((micros, seq_len, 2 * kv), BF),
        jax.ShapeDtypeStruct((micros, rows, heads), BF),
        jax.ShapeDtypeStruct((local, model, 2 * ff), BF),
        jax.ShapeDtypeStruct((local * ff, model), BF),
    )
    scratch = [
        pltpu.VMEM((seq_len, model), F32),
        pltpu.VMEM((seq_len, ff), F32),
        pltpu.VMEM((micros * rows, model), BF),
        pltpu.VMEM((micros, chunks, 4 * rows, LANES), BF),
        pltpu.VMEM((micros, seq_len, 2 * kv), BF),
        pltpu.VMEM((micros, rows, heads), BF),
        pltpu.VMEM((micros, rows, model), F32),
        pltpu.VMEM((micros, seq_len, LANES), F32),
        pltpu.VMEM((seq_len, LANES), F32),
        pltpu.VMEM((model, LANES), BF),
        pltpu.VMEM((micros, seq_len, model), BF),
        pltpu.VMEM((micros, seq_len, model), BF),
        pltpu.VMEM((micros, seq_len, local * ff), BF),
        pltpu.VMEM((micros * local, seq_len, 2 * ff), BF),
        pltpu.VMEM(w_out.shape, BF),
        pltpu.VMEM((local, model, 2 * ff), BF),
        pltpu.VMEM((local * ff, model), BF),
        pltpu.VMEM((seq_len, model), BF),
        pltpu.VMEM((count + 1, rows, model), BF),
        pltpu.VMEM((seq_len, wide_in), BF),
        pltpu.VMEM((count + 1, rows, wide_in), BF),
        pltpu.VMEM((rows, model), F32),
        pltpu.VMEM((micros, rows, wide_in), F32),
    ] + [dma((micros, 2, 2, steps))] * 5 + [dma((2 * split + 3,)), dma((2 * local + 5,))]
    dims = (micros, rows, count, local, ff, model)
    return pl.pallas_call(
        functools.partial(forward_kernel, dims),
        out_shape=out_shape,
        in_specs=[smem] + [vmem] * 8 + [hbm] * 5,
        out_specs=(vmem,) + (hbm,) * 7,
        scratch_shapes=scratch,
        name="layer_forward",
        compiler_params=pltpu.CompilerParams(
            collective_id=0, has_side_effects=True, vmem_limit_bytes=VMEM_LIMIT
        ),
    )(
        lengths, tokens, cot, routes, gain_one.reshape(1, -1), gain_two.reshape(1, -1),
        jnp.asarray(cos), jnp.asarray(sin), w_router, w_query, w_keyval, w_out, gate_up,
        down.reshape(local * ff, model),
    )


def norm_backward(grad_normed, inputs, scale_rows, gain_vec):
    scaled = grad_normed * gain_vec
    gain_grad = jnp.sum(grad_normed * inputs * scale_rows, 0)
    input_part = scale_rows * (
        scaled - inputs * scale_rows * scale_rows * jnp.mean(scaled * inputs, -1, keepdims=True)
    )
    return (input_part, gain_grad)


def plain_rope(rows, cos, sin):
    width = rows.shape[1]
    cos, sin = jnp.tile(cos, (1, width // LANES)), jnp.tile(sin, (1, width // LANES))
    grouped = rows.reshape(rows.shape[0], -1, 2, HEAD_DIM // 2)
    return rows * cos + grouped[:, :, ::-1].reshape(rows.shape) * sin


def on_device(
    tokens, lengths, routes, attn_gain, w_query, w_keyval, w_out, ffn_gain, w_router,
    expert_gate_up, expert_down, cotangent,
):
    count = lax.axis_size("expert")
    z = lax.axis_index("expert")
    micros, _, rows, model = tokens.shape
    seq_len = routes.shape[2]
    experts = w_router.shape[1]
    local, ff = expert_gate_up.shape[0], expert_down.shape[1]
    kv = w_keyval.shape[1] // 2
    chunks = kv // LANES
    y, hidden, moe, queries, keyval, mixture, grad_gu, grad_dn = forward_call(
        count, tokens, lengths, routes, attn_gain, w_query, w_keyval, w_out, ffn_gain, w_router,
        expert_gate_up, expert_down, cotangent,
    )
    cos, sin = rope_constants(seq_len)
    cos = lax.dynamic_slice_in_dim(jnp.asarray(cos), z * rows, rows, 0)
    sin = lax.dynamic_slice_in_dim(jnp.asarray(sin), z * rows, rows, 0)
    local_pos = z * rows + jnp.arange(rows, dtype=jnp.int32)
    all_pos = jnp.arange(seq_len, dtype=jnp.int32)
    low = jnp.arange(LANES) < HEAD_DIM
    roll = lambda v: jnp.roll(v, HEAD_DIM, -1)
    sums = [0.0] * 6
    input_grads = []
    for m in range(micros):
        length = lengths[m, 0]
        live = (local_pos < length)[:, None]
        x_rows = tokens[m, 0].astype(F32)
        scale_one = rms_scale(x_rows)
        normed = (x_rows * scale_one * attn_gain).astype(BF)
        scale_two = rms_scale(hidden[m])
        normed2 = (hidden[m] * scale_two * ffn_gain).astype(BF)
        logits = nn(normed2, w_router)
        ids = lax.dynamic_slice_in_dim(routes[m, 0], z * rows, rows, 0)
        named = (ids[:, :, None] == jnp.arange(experts)).any(1) & live
        masked = jnp.where(named, logits, NEG_FILL)
        raised = jnp.where(named, jnp.exp(masked - masked.max(-1, keepdims=True)), 0.0)
        total = raised.sum(-1, keepdims=True)
        gate = raised / jnp.where(total > 0, total, 1.0)
        d_gate = moe[m, :, model : model + experts]
        d_logits = (gate * (d_gate - jnp.sum(gate * d_gate, -1, keepdims=True))).astype(BF)
        d_normed2 = moe[m, :, :model] + nt(d_logits, w_router)
        part, gain_two = norm_backward(d_normed2, hidden[m], scale_two, ffn_gain)
        d_hidden = cotangent[m, 0].astype(F32) + part
        d_attn = jnp.where(live, d_hidden, 0.0).astype(BF)
        d_mix = nt(d_attn, w_out).astype(BF)
        d_query, d_key, d_value = [], [], []
        for i in range(chunks):
            lanes = slice(i * LANES, (i + 1) * LANES)
            key, value = keyval[m, :, lanes], keyval[m, :, kv + i * LANES : kv + (i + 1) * LANES]
            first, second = (
                d_mix[:, c * LANES : (c + 1) * LANES] for c in (2 * i, 2 * i + 1)
            )
            d_stack = jnp.concatenate(
                [
                    jnp.where(low, first, 0), jnp.where(low, roll(first), 0),
                    jnp.where(low, 0, roll(second)), jnp.where(low, 0, second),
                ]
            ).astype(BF)
            s = nt(queries[m, i], key) * ATTENTION_SCALE
            ok = (all_pos[None, :] <= jnp.tile(local_pos, 4)[:, None]) & (all_pos < length)[None, :]
            prob = jax.nn.softmax(jnp.where(ok, s, NEG_FILL), axis=-1)
            d_prob = nt(d_stack, value)
            d_scores = (prob * (d_prob - jnp.sum(prob * d_prob, -1, keepdims=True))).astype(BF)
            dq = nn(d_scores, key) * ATTENTION_SCALE
            d_key.append(tn(d_scores, queries[m, i]) * ATTENTION_SCALE)
            d_value.append(tn(prob.astype(BF), d_stack))
            q = [dq[k * rows : (k + 1) * rows] for k in range(4)]
            d_query += [jnp.where(low, q[0], roll(q[1])), jnp.where(low, roll(q[2]), q[3])]
        d_query = plain_rope(jnp.concatenate(d_query, 1), cos, -sin).astype(BF)
        d_kv = lax.psum_scatter(
            jnp.concatenate(d_key + d_value, 1).astype(BF), "expert", scatter_dimension=0, tiled=True
        ).astype(F32)
        d_kv = jnp.concatenate([plain_rope(d_kv[:, :kv], cos, -sin), d_kv[:, kv:]], 1).astype(BF)
        d_normed = nt(d_query, w_query) + nt(d_kv, w_keyval)
        part, gain_one = norm_backward(d_normed, x_rows, scale_one, attn_gain)
        input_grads.append(d_hidden + part)
        terms = (
            gain_one, tn(normed, d_query), tn(normed, d_kv), tn(mixture[m], d_attn), gain_two,
            tn(normed2, d_logits),
        )
        sums = [a + b for a, b in zip(sums, terms)]
    both = ("dp", "expert")
    scatter = lambda v: lax.psum_scatter(v, both, scatter_dimension=0, tiled=True)
    dense = [
        scatter(v if k in (0, 4, 5) else v.astype(BF)).astype(F32) for k, v in enumerate(sums)
    ]
    spread = lambda v: lax.psum_scatter(v, "dp", scatter_dimension=1, tiled=True).astype(F32)
    return (
        y, jnp.stack(input_grads)[:, None], *dense, spread(grad_gu),
        spread(grad_dn.reshape(local, ff, model)),
    )


def solution(mesh):
    placed = (
        P(None, "dp", "expert", None), P(None, "dp"), P(None, "dp", None, None), P(), P(), P(), P(),
        P(), P(), P("expert", None, None), P("expert", None, None), P(None, "dp", "expert", None),
    )
    return jax.shard_map(
        on_device,
        mesh=mesh,
        in_specs=placed,
        out_specs=(
            P(None, "dp", "expert", None), P(None, "dp", "expert", None), P(("dp", "expert")),
            P(("dp", "expert"), None), P(("dp", "expert"), None), P(("dp", "expert"), None),
            P(("dp", "expert")), P(("dp", "expert"), None), P("expert", "dp", None),
            P("expert", "dp", None),
        ),
        check_vma=False,
    )
```

time: 1740 us -> 1050 us (0.60)
  local copies, waits for them, and re-layouts: 392 us -> 34.3 us
  waiting for transfers between devices: 953 us -> 601 us
  Pallas kernels: 0 us -> 243 us
  other arithmetic: 130 us -> 32.8 us
  matrix products: 152 us -> 77 us
  starting transfers between devices: 53.1 us -> 0.9 us
    all_to_all x10 -> x0, waiting for transfers between devices: 336 us -> none  [the longest x2 181 us: on_device(): lax.all_to_all(grad_inputs, 'expert', split_axis=0, concat_axis=0, tiled=...]
    gather x34 -> x0, local copies, waits for them, and re-layouts: 253 us -> none  [the longest x10 199 us: expert_forward(): chosen = jnp.take_along_axis(logits, route_table, axis=-1)]
    pallas_call x0 -> x1, Pallas kernels: none -> 243 us  [forward_call(): pl.pallas_call(functools.partial(forward_kernel, dims), out_shape=out_sha...]
    unnamed x295 -> x166, local copies, waits for them, and re-layouts: 93.6 us -> 15.9 us
    dot_general x50 -> x58, matrix products: 152 us -> 77 us  [dot_of(): lax.dot_general(left, right, (((left_dim,), (right_dim,)), ((), ())), pre...]
    scatter-add x4 -> x0, other arithmetic: 60.4 us -> none  [the longest x2 30.9 us: on_device(): moe_grad = jnp.zeros((local_rows + 1, model_width), jnp.float32).at[flat_...]
    all_to_all x10 -> x0, starting transfers between devices: 51.5 us -> none  [the longest x2 11.9 us: on_device(): lax.all_to_all(outgoing, 'expert', split_axis=0, concat_axis=0, tiled=True)]
    reduce_scatter x5 -> x7, waiting for transfers between devices: 519 us -> 488 us  [the longest x3 364 us: on_device(): lax.psum_scatter(v, both, scatter_dimension=0, tiled=True)]
  transfers between devices with their start and end apart: 20 -> 8, of which waited for: 11 -> 6; matrix products, arithmetic and copies ran while one was open for 34% -> 9% of each run, Pallas kernels for 0% -> 0%
where the time goes in v1:
time: 1050 us; the launch traced here: 1040 us
  waiting for transfers between devices  601 us (57%)
  Pallas kernels  243 us (23%)
  matrix products  77 us (7%)
  blocking collectives  37.3 us (4%)
  local copies, waits for them, and re-layouts  34.3 us (3%)
  other arithmetic  32.8 us (3%)
  between operations  15.8 us (2%)
    reduce_scatter x3, waiting for transfers between devices, on_device(): lax.psum_scatter(v, both, scatter_dimension=0, tiled=True)  364 us
    pallas_call x1, Pallas kernels, forward_call(): pl.pallas_call(functools.partial(forward_kernel, dims), out_shape=out_sha...  243 us
    reduce_scatter x2, waiting for transfers between devices, on_device(): lax.psum_scatter(v, 'dp', scatter_dimension=1, tiled=True).astype(F32)  124 us
    unnamed x9, waiting for transfers between devices  113 us
    dot_general x58, matrix products, dot_of(): lax.dot_general(left, right, (((left_dim,), (right_dim,)), ((), ())), pre...  77 us
    unnamed x1, blocking collectives  37.3 us
  transfers between devices with their start and end apart: 8, of which 6 were waited for; matrix products, arithmetic and copies ran while one was open for 9% of the time, Pallas kernels for 0%

profile of v1, /device:TPU:0, one launch (start us, length us, event | category | flops | bytes accessed | tf_op | source)
XLA Modules:
  0.0 1042.5 jit_solution(8234615008492478537)
XLA Ops:
  14.6 243.0 %layer_forward.1 = (bf16[2,1,128,1024]{3,2,1,0:T(8,128)(2,1)}, f32[2,128,1024]{2,1,0:T(8,128)}, f32[2,128,1152]{2,1,0:T(8,128)}, bf16[2,4,512,128]{3,2,1,0:T(8,1...) custom-call(s32[2,1]{1,0:T(2,128)} %copy.156.lengths, ...), custom_call_target="tpu_custom_call" | custom-call | tf_op jit(solution)/shard_map/layer_forward/pallas_call | solution.py:695
  257.6 2.4 fusion.284
  260.0 2.3 fusion.283
  262.3 3.0 fusion.282
  265.3 2.9 fusion.281
  324.8 2.1 add_convert_fusion
  349.3 2.1 add_convert_fusion.3
  353.7 2.1 add_convert_fusion.2
  359.8 2.1 add_convert_fusion.1
  365.4 1.8 tile.21.clone
  367.2 2.0 copy.170
  369.2 2.1 copy.169
  371.3 2.0 copy.189
  373.4 3.3 fusion.102
  378.4 111.8 %reduce-scatter.25.cloned.1.call-done = f32[32,16]{1,0:T(8,128)} async-done(((f32[1024,16]{1,0:T(8,128)}), f32[32,16]{1,0:T(8,128)}) %reduce-scatter.25.cloned.1.call-update) | async-done | bytes 2064
  491.5 2.6 convolution_add_fusion.2
  495.9 37.3 %all-reduce.2 = (f32[1024]{0:T(1024)S(1)}, f32[1024]{0:T(1024)S(1)}) all-reduce(f32[1024]{0:T(1024)S(1)} %add.170, f32[1024]{0:T(1024)S(1)} %add.176), channel_id=4, replica_groups=mesh['dp'=8,'expert'=4] {'dp','expert'}, use_global_device_ids=true, to_apply=%region_44.45.clone | all-reduce | flops 2048 | bytes 16384
  537.2 90.3 %reduce-scatter.19.cloned.1.call-done = bf16[32,1024]{1,0:T(8,128)(2,1)} async-done(((bf16[1024,1024]{1,0:T(8,128)(2,1)}), bf16[32,1024]{1,0:T(8,128)(2,1)}) %reduce-scatter.19.cloned.1.call-update) | async-done | bytes 65552 | tf_op jit(solution)/shard_map/reduce_scatter | solution.py:812
  629.1 136.7 %reduce-scatter.15.cloned.1.call-done = bf16[32,1024]{1,0:T(8,128)(2,1)} async-done(((bf16[1024,1024]{1,0:T(8,128)(2,1)}), bf16[32,1024]{1,0:T(8,128)(2,1)}) %reduce-scatter.15.cloned.1.call-update) | async-done | bytes 65552 | tf_op jit(solution)/shard_map/reduce_scatter | solution.py:812
  767.3 136.5 %reduce-scatter.17.cloned.1.call-done = bf16[32,1024]{1,0:T(8,128)(2,1)} async-done(((bf16[1024,1024]{1,0:T(8,128)(2,1)}), bf16[32,1024]{1,0:T(8,128)(2,1)}) %reduce-scatter.17.cloned.1.call-update) | async-done | bytes 65552 | tf_op jit(solution)/shard_map/reduce_scatter | solution.py:812
  905.3 51.4 %reduce-scatter.23.cloned.1.call-done = bf16[4,64,1024]{2,1,0:T(8,128)(2,1)} async-done(((bf16[4,512,1024]{2,1,0:T(8,128)(2,1)}), bf16[4,64,1024]{2,1,0:T(8,128)(2,1)}) %reduce-scatter.23.cloned.1.call-update) | async-done | bytes 524304 | tf_op jit(solution)/shard_map/reduce_scatter | solution.py:816
  956.7 2.1 convert_element_type.267
  958.8 73.0 %reduce-scatter.21.cloned.1.call-done = bf16[4,128,1024]{2,1,0:T(8,128)(2,1)} async-done(((bf16[4,1024,1024]{2,1,0:T(8,128)(2,1)}), bf16[4,128,1024]{2,1,0:T(8,128)(2,1)}) %reduce-scatter.21.cloned.1.call-update) | async-done | bytes 1048592 | tf_op jit(solution)/shard_map/reduce_scatter | solution.py:816
  1031.9 2.8 convert_element_type.266
  (337 shorter events, 108.9 us)
Async XLA Ops:
  7.2 348.8 %reduce-scatter.13.cloned.1.call-start = ((), (), s32[]{:S(2)}) async-start(), calls=%async_computation.9 | async-start | bytes 1310720 | tf_op jit(solution)/shard_map/reduce_scatter | solution.py:799
  13.0 252.3 %copy-start.63 = (s32[512]{0:T(512)}, s32[512]{0:T(512)S(1)}, u32[]{:S(2)}) copy-start(s32[512]{0:T(512)S(1)} %broadcast_bitcast_fusion) | copy-start | bytes 6148
  262.3 7.5 copy-start.3
  262.3 7.6 copy-start.44
  262.3 7.7 copy-start.48
  269.9 6.3 copy-start.61
  276.6 46.4 %copy-start.5 = (f32[128,1024]{1,0:T(8,128)}, f32[128,1024]{1,0:T(8,128)S(1)}, u32[]{:S(2)}) copy-start(f32[128,1024]{1,0:T(8,128)S(1)} %get-tuple-element.118) | copy-start | bytes 1572868
  299.0 58.3 %reduce-scatter.11.cloned.1.call-start = ((), (), s32[]{:S(2)}) async-start(), calls=%async_computation.8 | async-start | bytes 1310720 | tf_op jit(solution)/shard_map/reduce_scatter | solution.py:799
  320.5 169.6 %reduce-scatter.25.cloned.1.call-start = ((), (), s32[]{:S(2)}) async-start(), calls=%async_computation.15 | async-start | bytes 540672
  323.0 304.6 %reduce-scatter.19.cloned.1.call-start = ((), (), s32[]{:S(2)}) async-start(), calls=%async_computation.12 | async-start | bytes 2162688 | tf_op jit(solution)/shard_map/reduce_scatter | solution.py:812
  327.0 6.4 copy-start.26
  327.0 438.8 %reduce-scatter.15.cloned.1.call-start = ((), (), s32[]{:S(2)}) async-start(), calls=%async_computation.10 | async-start | bytes 2162688 | tf_op jit(solution)/shard_map/reduce_scatter | solution.py:812
  328.0 6.6 copy-start.29
  352.9 6.9 copy-start.54
  355.9 547.9 %reduce-scatter.17.cloned.1.call-start = ((), (), s32[]{:S(2)}) async-start(), calls=%async_computation.11 | async-start | bytes 2162688 | tf_op jit(solution)/shard_map/reduce_scatter | solution.py:812
  362.0 594.7 %reduce-scatter.23.cloned.1.call-start = ((), (), s32[]{:S(2)}) async-start(), calls=%async_computation.14 | async-start | bytes 4718592 | tf_op jit(solution)/shard_map/reduce_scatter | solution.py:816
  362.7 669.1 %reduce-scatter.21.cloned.1.call-start = ((), (), s32[]{:S(2)}) async-start(), calls=%async_computation.13 | async-start | bytes 9437184 | tf_op jit(solution)/shard_map/reduce_scatter | solution.py:816
  365.4 8.0 copy-start.1
  378.3 115.7 %copy-start.4 = (bf16[1024,1024]{1,0:T(8,128)(2,1)S(1)}, bf16[1024,1024]{1,0:T(8,128)(2,1)}, u32[]{:S(2)}) copy-start(bf16[1024,1024]{1,0:T(8,128)(2,1)} %keyval_hbm.1) | copy-start | bytes 6291460
  378.3 115.7 %copy-start.40 = (bf16[128,512]{1,0:T(8,128)(2,1)S(1)}, bf16[128,512]{1,0:T(8,128)(2,1)}, u32[]{:S(2)}) copy-start(bf16[128,512]{1,0:T(8,128)(2,1)} %copy-done.39) | copy-start | bytes 393220
  378.3 115.7 %copy-start.55 = (f32[128]{0:T(128)S(1)}, f32[128]{0:T(128)}, u32[]{:S(2)}) copy-start(f32[128]{0:T(128)} %copy-done.54) | copy-start | bytes 1540
  378.4 115.8 %copy-start.57 = (f32[128]{0:T(128)S(1)}, f32[128]{0:T(128)}, u32[]{:S(2)}) copy-start(f32[128]{0:T(128)} %copy-done.56) | copy-start | bytes 1540
  494.1 40.3 %copy-start.58 = (f32[128]{0:T(128)S(1)}, f32[128]{0:T(128)}, u32[]{:S(2)}) copy-start(f32[128]{0:T(128)} %copy-done.56) | copy-start | bytes 1540
  905.3 129.3 %copy-start.43 = (bf16[2,1,128,1024]{3,2,1,0:T(8,128)(2,1)S(1)}, bf16[2,1,128,1024]{3,2,1,0:T(8,128)(2,1)}, u32[]{:S(2)}) copy-start(bf16[2,1,128,1024]{3,2,1,0:T(8,128)(2,1)} %get-tuple-element.290) | copy-start | bytes 1572868
  (55 other events, 143.4 us)
Sparse Core Ops, SparseCore 0:
  299.1 26.7 reduce-scatter.12
  328.9 25.7 reduce-scatter.10
  356.9 133.1 reduce-scatter.24
  492.3 135.1 reduce-scatter.18
  630.2 135.5 reduce-scatter.14
  768.0 135.7 reduce-scatter.16
  907.2 49.4 reduce-scatter.22
  960.5 71.2 reduce-scatter.20

commit v2 on v1

--- a/solution.py
+++ b/solution.py
@@ -18,7 +18,7 @@
 STRIP = 16
 BF = jnp.bfloat16
 F32 = jnp.float32
-VMEM_LIMIT = 62 * 2**20
+VMEM_LIMIT = 63 * 2**20
 
 
 def dot_of(left, right, left_dim, right_dim):
@@ -171,7 +171,7 @@
     def place(self, way, slot, z):
         if way == 0:
             return slot - (z - 1)
-        return self.count - (slot - (self.count - 2 - z))
+        return self.count - (slot - (self.count - 2 - z)) - (2 if self.ways == [1] else 0)
 
     def copy(self, way, slot, block):
         z = lax.axis_index("expert")
@@ -709,20 +709,572 @@
     )
 
 
-def norm_backward(grad_normed, inputs, scale_rows, gain_vec):
-    scaled = grad_normed * gain_vec
-    gain_grad = jnp.sum(grad_normed * inputs * scale_rows, 0)
-    input_part = scale_rows * (
-        scaled - inputs * scale_rows * scale_rows * jnp.mean(scaled * inputs, -1, keepdims=True)
+def plane_of(devices):
+    side = math.isqrt(devices // 2)
+    return side, side
+
+
+def device_at(plane, y, x, core):
+    return {"dp": (y * plane[1] + x) * 2 + core}
+
+
+class PlaneReduce:
+    def __init__(self, plane, source, own, total, first_land, second_land, x_first, sems, local=None):
+        self.plane, self.source, self.own, self.total = plane, source, own, total
+        self.lands, self.x_first, self.sems, self.local = (first_land, second_land), x_first, sems, local
+        index = lax.axis_index("dp")
+        self.core = lax.rem(index, 2)
+        chip = index // 2
+        self.y, self.x = chip // plane[1], lax.rem(chip, plane[1])
+
+    def remote(self, src, dst, number, where):
+        return pltpu.make_async_remote_copy(
+            src_ref=src,
+            dst_ref=dst,
+            send_sem=self.sems.at[0, number],
+            recv_sem=self.sems.at[1, number],
+            device_id=device_at(self.plane, *where),
+            device_id_type=pl.DeviceIdType.MESH,
+        )
+
+    def sibling(self):
+        return self.remote(
+            self.source.at[:, :, 1 - self.core], self.total, 0, (self.y, self.x, 1 - self.core)
+        )
+
+    def start(self):
+        self.sibling().start()
+
+    def along(self, stage):
+        return self.x_first == (stage == 0)
+
+    def hops(self, stage):
+        along_x = self.along(stage)
+        size = self.plane[1] if along_x else self.plane[0]
+        base = 1 if stage == 0 else self.plane[1] if self.x_first else self.plane[0]
+        for k in range(1, size):
+            if along_x:
+                place = lax.rem(self.x + k, size)
+                where = (self.y, place, self.core)
+                view = (
+                    self.total.at[:, place] if stage == 0 else self.total.at[self.y, place]
+                )
+            else:
+                place = lax.rem(self.y + k, size)
+                where = (place, self.x, self.core)
+                view = self.total.at[place] if stage == 0 else self.total.at[place, self.x]
+            yield k, self.remote(view, self.lands[stage].at[k - 1], base + k - 1, where)
+
+    def send(self, stage):
+        for _, copy in self.hops(stage):
+            copy.start()
+
+    def pair_sum(self):
+        if self.local is not None:
+            self.local.wait()
+        self.sibling().wait_recv()
+        count = self.plane[0] * self.plane[1]
+        for b in range(count):
+            y, x = b // self.plane[1], b % self.plane[1]
+            own = self.own[y, x] if self.local is not None else self.source[y, x, self.core]
+            self.total[y, x] = (self.total[y, x].astype(F32) + own.astype(F32)).astype(BF)
+
+    def take(self, stage):
+        land = self.lands[stage]
+        for k, copy in self.hops(stage):
+            copy.wait_recv()
+        if stage == 0:
+            for other in range(self.plane[0] if self.x_first else self.plane[1]):
+                where = (other, self.x) if self.x_first else (self.y, other)
+                summed = self.total[where].astype(F32)
+                for k in range(land.shape[0]):
+                    summed = summed + land[k, other].astype(F32)
+                self.total[where] = summed.astype(BF)
+            return None
+        summed = self.total[self.y, self.x].astype(F32)
+        for k in range(land.shape[0]):
+            summed = summed + land[k].astype(F32)
+        return summed
+
+    def finish(self):
+        self.sibling().wait_send()
+        for stage in range(2):
+            for _, copy in self.hops(stage):
+                copy.wait_send()
+
+
+class LineReduce:
+    def __init__(self, parts, land, rows, count, sems):
+        self.parts, self.land, self.rows, self.count, self.sems = parts, land, rows, count, sems
+        self.group = max(rows, STRIP)
+
+    def span(self, z):
+        if self.group == self.rows:
+            return rows_at(z, self.rows)
+        return pl.ds(pl.multiple_of(z * self.rows // self.group * self.group, self.group), self.group)
+
+    def hops(self):
+        z = lax.axis_index("expert")
+        for k in range(1, self.count):
+            target = lax.rem(z + k, self.count)
+            yield k, pltpu.make_async_remote_copy(
+                src_ref=self.parts.at[self.span(target), :],
+                dst_ref=self.land.at[k - 1],
+                send_sem=self.sems.at[0, k - 1],
+                recv_sem=self.sems.at[1, k - 1],
+                device_id={"expert": target},
+                device_id_type=pl.DeviceIdType.MESH,
+            )
+
+    def start(self):
+        for _, copy in self.hops():
+            copy.start()
+
+    def total(self):
+        for _, copy in self.hops():
+            copy.wait_recv()
+        summed = self.parts[self.span(lax.axis_index("expert")), :].astype(F32)
+        for k in range(self.count - 1):
+            summed = summed + self.land[k].astype(F32)
+        return summed
+
+    def finish(self):
+        for _, copy in self.hops():
+            copy.wait_send()
+
+
+def full_barrier(plane, count):
+    index = lax.axis_index("dp")
+    z = lax.axis_index("expert")
+    core, chip = lax.rem(index, 2), index // 2
+    y, x = chip // plane[1], lax.rem(chip, plane[1])
+    barrier = pltpu.get_barrier_semaphore()
+    greeted = [device_at(plane, y, x, 1 - core)]
+    greeted += [device_at(plane, y, lax.rem(x + k, plane[1]), core) for k in range(1, plane[1])]
+    greeted += [device_at(plane, lax.rem(y + k, plane[0]), x, core) for k in range(1, plane[0])]
+    greeted += [{"expert": lax.rem(z + k, count)} for k in range(1, count)]
+    for device in greeted:
+        pl.semaphore_signal(barrier, inc=1, device_id=device, device_id_type=pl.DeviceIdType.MESH)
+    pl.semaphore_wait(barrier, len(greeted))
+
+
+def backward_kernel(
+    dims,
+    plane,
+    lengths,
+    tokens,
+    cot,
+    routes,
+    gain_one,
+    gain_two,
+    cos_ref,
+    sin_ref,
+    router,
+    hidden,
+    moe,
+    queries,
+    keyval,
+    mixture,
+    query_hbm,
+    keyval_hbm,
+    out_hbm,
+    grad_gu,
+    grad_dn,
+    input_grad,
+    gu_out,
+    dn_out,
+    dense_out,
+    small_out,
+    w_query,
+    w_keyval,
+    w_out,
+    router_pad,
+    normed,
+    normed2,
+    d_attn,
+    d_mix,
+    d_query,
+    d_keyval,
+    d_logits,
+    wide,
+    d_hidden,
+    gains,
+    scores,
+    d_probs,
+    probs,
+    d_scores,
+    stacked,
+    kv_parts,
+    kv_land,
+    kv_own,
+    gu_own,
+    gu_sum,
+    gu_land_a,
+    gu_land_b,
+    dn_own,
+    dn_sum,
+    dn_land_a,
+    dn_land_b,
+    grads,
+    grads_sum,
+    grads_land_a,
+    grads_land_b,
+    grads_line,
+    grads_line_land,
+    small,
+    small_sum,
+    small_land_a,
+    small_land_b,
+    small_line,
+    small_line_land,
+    gu_sems,
+    dn_sems,
+    grads_sems,
+    small_sems,
+    line_sems,
+    kv_sems,
+    load_sems,
+    own_sems,
+):
+    micros, rows, count, local, ff, model = dims
+    seq_len = count * rows
+    kv = keyval.shape[2] // 2
+    chunks = kv // LANES
+    both = micros * rows
+    z = lax.axis_index("expert")
+    row_base = z * rows
+    block = small_line.shape[0] // count
+    core = lax.rem(lax.axis_index("dp"), 2)
+
+    loads = []
+    for number, (src, dst) in enumerate(
+        ((out_hbm, w_out), (query_hbm, w_query), (keyval_hbm, w_keyval))
+    ):
+        loads.append(pltpu.make_async_copy(src, dst, load_sems.at[number]))
+        loads[-1].start()
+    full_barrier(plane, count)
+
+    experts = []
+    for j in range(local):
+        for kind, (source, own, total, land_a, land_b, sems) in enumerate(
+            (
+                (grad_gu, gu_own, gu_sum, gu_land_a, gu_land_b, gu_sems),
+                (grad_dn, dn_own, dn_sum, dn_land_a, dn_land_b, dn_sems),
+            )
+        ):
+            load = pltpu.make_async_copy(
+                source.at[j, :, :, core], own.at[j % 2], own_sems.at[2 * j + kind]
+            )
+            item = PlaneReduce(
+                plane, source.at[j], own.at[j % 2], total.at[j], land_a.at[j], land_b.at[j],
+                j % 2 == 0, sems.at[j], load,
+            )
+            item.start()
+            if j < 2:
+                load.start()
+            experts.append(item)
+    dense = [
+        PlaneReduce(
+            plane, grads.at[k], None, grads_sum.at[k], grads_land_a.at[k], grads_land_b.at[k],
+            k % 2 == 0, grads_sems.at[k],
+        )
+        for k in range(6)
+    ]
+    dense.append(
+        PlaneReduce(
+            plane, small, None, small_sum, small_land_a, small_land_b, True, small_sems
+        )
     )
-    return (input_part, gain_grad)
-
-
-def plain_rope(rows, cos, sin):
-    width = rows.shape[1]
-    cos, sin = jnp.tile(cos, (1, width // LANES)), jnp.tile(sin, (1, width // LANES))
-    grouped = rows.reshape(rows.shape[0], -1, 2, HEAD_DIM // 2)
-    return rows * cos + grouped[:, :, ::-1].reshape(rows.shape) * sin
+    lines = [
+        LineReduce(grads_line.at[k], grads_line_land.at[k], block, count, line_sems.at[k])
+        for k in range(6)
+    ] + [LineReduce(small_line, small_line_land, block, count, line_sems.at[6])]
+    reduce_kv = [
+        Reduce(kv_parts.at[m], kv_land.at[m], rows, count, kv_sems.at[m], up=False)
+        for m in range(micros)
+    ]
+
+    queue = []
+
+    def advance(amount=1):
+        for _ in range(amount):
+            if queue:
+                queue.pop(0)()
+
+    def paired(item):
+        item.pair_sum()
+        item.send(0)
+
+    def crossed(item):
+        item.take(0)
+        item.send(1)
+
+    def expert_done(number):
+        out = gu_out if number % 2 == 0 else dn_out
+        out[number // 2] = experts[number].take(1)
+
+    def dense_done(number):
+        ref = grads_line.at[number] if number < 6 else small_line
+        ref[...] = dense[number].take(1).astype(BF)
+        lines[number].start()
+
+    def line_done(number):
+        if number < 6:
+            half = model // 2
+            dense_out[number // 2, :, (number % 2) * half : (number % 2 + 1) * half] = lines[
+                number
+            ].total()
+        else:
+            small_out[...] = lines[number].total()
+
+    def put_grads(number, left, right):
+        half = model // 2
+        shape = grads.shape[1:]
+        for k in range(2):
+            value = tn(left, right[:, k * half : (k + 1) * half])
+            grads[2 * number + k] = value.astype(BF).reshape(shape)
+            dense[2 * number + k].start()
+
+    def part(function, *values):
+        return functools.partial(function, *values)
+
+    def expert_paired(number):
+        paired(experts[number])
+        if number + 4 < len(experts):
+            experts[number + 4].local.start()
+
+    queue += [part(expert_paired, number) for number in range(len(experts))]
+
+    router_pad[...] = jnp.zeros(router_pad.shape, BF)
+    router_pad[:, 0 : router.shape[1]] = router[...]
+    gains[...] = jnp.zeros(gains.shape, F32)
+
+    def norm_back(d_rows, inputs, scale, gain, row):
+        scaled = d_rows * gain
+        gains[row : row + 1, :] += jnp.sum(d_rows * inputs * scale, 0, keepdims=True)
+        return scale * (
+            scaled - inputs * scale * scale * jnp.mean(scaled * inputs, -1, keepdims=True)
+        )
+
+    def live_rows(m):
+        return (row_base + lax.broadcasted_iota(jnp.int32, (rows, 1), 0)) < lengths[m, 0]
+
+    router_lanes = router.shape[1]
+    for m in range(micros):
+        span = slice(m * rows, (m + 1) * rows)
+        x_rows = tokens[m, 0].astype(F32)
+        normed[span, :] = (x_rows * rms_scale(x_rows) * gain_one[...]).astype(BF)
+        v = hidden[m]
+        scale = rms_scale(v)
+        normed2[span, :] = (v * scale * gain_two[...]).astype(BF)
+        logits = nn(normed2[span, :], router_pad[...])
+        lane = lane_ids(rows)
+        ids = routes[m, 0, rows_at(z, rows), :]
+        hit = jnp.zeros((rows, LANES), F32)
+        for k in range(routes.shape[3]):
+            hit = hit + (ids[:, k : k + 1] == lane).astype(F32)
+        live = live_rows(m)
+        on = jnp.where(live, hit, 0.0) > 0.0
+        masked = jnp.where(on, logits, NEG_FILL)
+        raised = jnp.where(on, jnp.exp(masked - jnp.max(masked, -1, keepdims=True)), 0.0)
+        total = jnp.sum(raised, -1, keepdims=True)
+        gate = raised / jnp.where(total > 0.0, total, 1.0)
+        d_gate = moe[m, :, model:]
+        d_logits[span, :] = (
+            gate * (d_gate - jnp.sum(gate * d_gate, -1, keepdims=True))
+        ).astype(BF)
+        d_rows = moe[m, :, 0:model] + nt(d_logits[span, :], router_pad[...])
+        grown = cot[m, 0].astype(F32) + norm_back(
+            d_rows, v, scale, gain_two[...], router_lanes + 1
+        )
+        d_hidden[span, :] = grown
+        d_attn[span, :] = jnp.where(live, grown, 0.0).astype(BF)
+
+    loads[0].wait()
+    d_mix[...] = nt(d_attn[...], w_out[...]).astype(BF)
+    put_grads(2, mixture[...].reshape(both, mixture.shape[2]), d_attn[...])
+    advance(2)
+    cos = cos_ref[rows_at(z, rows), :]
+    sin = sin_ref[rows_at(z, rows), :]
+
+    def attend_back(m):
+        length = lengths[m, 0]
+        span = slice(m * rows, (m + 1) * rows)
+        for i in range(chunks):
+            lanes = slice(i * LANES, (i + 1) * LANES)
+            value_lanes = slice(kv + i * LANES, kv + (i + 1) * LANES)
+            pair = [
+                d_mix[span, c * LANES : (c + 1) * LANES].astype(F32) for c in (2 * i, 2 * i + 1)
+            ]
+            for k, rows_of in enumerate(stack_heads(*pair)):
+                stacked[k * rows : (k + 1) * rows, :] = rows_of.astype(BF)
+            scores[...] = nt(queries[m, i], keyval[m, :, lanes])
+            d_probs[...] = nt(stacked[...], keyval[m, :, value_lanes])
+
+            def strip_step(strip, carry):
+                where = rows_at(strip, STRIP)
+                prob = softmax_rows(
+                    masked_scores(scores, strip, rows, seq_len, row_base, length)
+                )
+                d_prob = d_probs[where, :]
+                delta = jnp.sum(prob * d_prob, -1, keepdims=True)
+                d_scores[where, :] = (prob * (d_prob - delta)).astype(BF)
+                probs[where, :] = prob.astype(BF)
+                return carry
+
+            lax.fori_loop(0, 4 * rows // STRIP, strip_step, 0)
+            turned = nn(d_scores[...], keyval[m, :, lanes]) * ATTENTION_SCALE
+            first, second = unstack_heads(turned, rows)
+            for c, chunk in ((2 * i, first), (2 * i + 1, second)):
+                d_query[span, c * LANES : (c + 1) * LANES] = rope(chunk, cos, -sin).astype(BF)
+            kv_parts[m, :, lanes] = (
+                tn(d_scores[...], queries[m, i]) * ATTENTION_SCALE
+            ).astype(BF)
+            kv_parts[m, :, value_lanes] = tn(probs[...], stacked[...]).astype(BF)
+            if i % 2 == 1:
+                advance()
+
+    slots = []
+    for m in range(micros):
+        attend_back(m)
+        reduce_kv[m].slot(0)
+    while queue:
+        advance()
+    for k in (4, 5):
+        paired(dense[k])
+    loads[1].wait()
+    put_grads(0, normed[...], d_query[...])
+    wide[...] = nt(d_query[...], w_query[...])
+    for slot in range(1, count):
+        for m in range(micros):
+            queue.append(part(reduce_kv[m].slot, slot))
+    first_wave = [part(crossed, item) for item in experts]
+    for k, item in enumerate(first_wave):
+        item()
+        advance()
+        if k == 1:
+            for number in (0, 1):
+                paired(dense[number])
+    while queue:
+        advance()
+    loads[2].wait()
+    for m in range(micros):
+        span = slice(m * rows, (m + 1) * rows)
+        reduce_kv[m].total(kv_own)
+        for c in range(chunks):
+            lanes = slice(c * LANES, (c + 1) * LANES)
+            d_keyval[span, lanes] = rope(kv_own[:, lanes], cos, -sin).astype(BF)
+        d_keyval[span, kv:] = kv_own[:, kv:].astype(BF)
+    put_grads(1, normed[...], d_keyval[...])
+    wide[...] += nt(d_keyval[...], w_keyval[...])
+    for m in range(micros):
+        span = slice(m * rows, (m + 1) * rows)
+        x_rows = tokens[m, 0].astype(F32)
+        input_grad[m, 0] = d_hidden[span, :] + norm_back(
+            wide[span, :], x_rows, rms_scale(x_rows), gain_one[...], router_lanes
+        )
+    small_value = tn(normed2[...], d_logits[...]) + gains[...].T
+    small[...] = small_value.astype(BF).reshape(small.shape)
+    dense[6].start()
+    for k in (2, 3, 6):
+        paired(dense[k])
+    for k in (4, 5, 0, 1):
+        crossed(dense[k])
+    for number in range(len(experts)):
+        expert_done(number)
+    for k in (4, 5, 0, 1):
+        dense_done(k)
+    for k in (2, 3, 6):
+        crossed(dense[k])
+    for k in (2, 3, 6):
+        dense_done(k)
+    for k in range(7):
+        line_done(k)
+    for item in experts + dense + lines + reduce_kv:
+        item.finish()
+
+
+def backward_call(
+    count, devices, tokens, lengths, routes, gain_one, w_query, w_keyval, w_out, gain_two,
+    w_router, cot, local, ff, hidden, moe, queries, keyval, mixture, grad_gu, grad_dn,
+):
+    micros, _, rows, model = tokens.shape
+    seq_len = routes.shape[2]
+    kv = w_keyval.shape[1] // 2
+    heads = w_query.shape[1]
+    plane = plane_of(devices)
+    block = model // devices // count
+    group = max(block, STRIP)
+    line = count * block
+    half = model // 2
+    both = micros * rows
+    cos, sin = rope_constants(seq_len)
+    gu_rows, dn_rows = model // devices, ff // devices
+    vmem = pl.BlockSpec(memory_space=pltpu.VMEM)
+    smem = pl.BlockSpec(memory_space=pltpu.SMEM)
+    hbm = pl.BlockSpec(memory_space=pl.ANY)
+    dma = pltpu.SemaphoreType.DMA
+    hops = plane[0] + plane[1] - 1
+
+    def reduce_scratch(lead, block_rows, width):
+        lead = tuple(lead)
+        return [
+            pltpu.VMEM(lead + plane + (block_rows, width), BF),
+            pltpu.VMEM(lead + (plane[1] - 1, plane[0], block_rows, width), BF),
+            pltpu.VMEM(lead + (plane[0] - 1, block_rows, width), BF),
+        ]
+
+    wide_bf = pltpu.VMEM((both, model), BF)
+    out_shape = (
+        jax.ShapeDtypeStruct((micros, 1, rows, model), F32),
+        jax.ShapeDtypeStruct((local, gu_rows, 2 * ff), F32),
+        jax.ShapeDtypeStruct((local, dn_rows, model), F32),
+        jax.ShapeDtypeStruct((3, group, model), F32),
+        jax.ShapeDtypeStruct((group, LANES), F32),
+    )
+    scratch = (
+        [pltpu.VMEM(w.shape, BF) for w in (w_query, w_keyval, w_out)]
+        + [pltpu.VMEM((model, LANES), BF)]
+        + [wide_bf, wide_bf, wide_bf, pltpu.VMEM((both, heads), BF), pltpu.VMEM((both, heads), BF)]
+        + [pltpu.VMEM((both, 2 * kv), BF), pltpu.VMEM((both, LANES), BF)]
+        + [pltpu.VMEM((both, model), F32)]
+        + [pltpu.VMEM((both, model), F32), pltpu.VMEM((LANES, model), F32)]
+        + [pltpu.VMEM((4 * rows, seq_len), F32)] * 2
+        + [pltpu.VMEM((4 * rows, seq_len), BF)] * 2
+        + [pltpu.VMEM((4 * rows, LANES), BF)]
+        + [pltpu.VMEM((micros, seq_len, 2 * kv), BF)]
+        + [pltpu.VMEM((micros, count - 1, rows, 2 * kv), BF), pltpu.VMEM((rows, 2 * kv), F32)]
+        + [pltpu.VMEM((2,) + plane + (gu_rows, 2 * ff), BF)]
+        + reduce_scratch((local,), gu_rows, 2 * ff)
+        + [pltpu.VMEM((2,) + plane + (dn_rows, model), BF)]
+        + reduce_scratch((local,), dn_rows, model)
+        + [pltpu.VMEM((6,) + plane + (2, line, half), BF)]
+        + reduce_scratch((6,), line, half)
+        + [pltpu.VMEM((6, line, half), BF), pltpu.VMEM((6, count - 1, group, half), BF)]
+        + [pltpu.VMEM(plane + (2, line, LANES), BF)]
+        + reduce_scratch((), line, LANES)
+        + [pltpu.VMEM((line, LANES), BF), pltpu.VMEM((count - 1, group, LANES), BF)]
+        + [dma((local, 2, hops)), dma((local, 2, hops)), dma((6, 2, hops)), dma((2, hops))]
+        + [dma((7, 2, count - 1)), dma((micros, 2, 2, count - 1)), dma((3,)), dma((2 * local,))]
+    )
+    dims = (micros, rows, count, local, ff, model)
+    return pl.pallas_call(
+        functools.partial(backward_kernel, dims, plane),
+        out_shape=out_shape,
+        in_specs=[smem] + [vmem] * 13 + [hbm] * 5,
+        out_specs=(vmem,) * 5,
+        scratch_shapes=scratch,
+        name="layer_backward",
+        compiler_params=pltpu.CompilerParams(
+            collective_id=1, has_side_effects=True, vmem_limit_bytes=VMEM_LIMIT
+        ),
+    )(
+        lengths, tokens, cot, routes, gain_one.reshape(1, -1), gain_two.reshape(1, -1),
+        jnp.asarray(cos), jnp.asarray(sin), w_router, hidden, moe, queries, keyval, mixture,
+        w_query, w_keyval, w_out,
+        grad_gu.reshape((local,) + plane + (2, gu_rows, 2 * ff)),
+        grad_dn.reshape((local,) + plane + (2, dn_rows, model)),
+    )
 
 
 def on_device(
@@ -730,93 +1282,26 @@
     expert_gate_up, expert_down, cotangent,
 ):
     count = lax.axis_size("expert")
-    z = lax.axis_index("expert")
-    micros, _, rows, model = tokens.shape
-    seq_len = routes.shape[2]
+    devices = lax.axis_size("dp")
+    model = tokens.shape[3]
     experts = w_router.shape[1]
     local, ff = expert_gate_up.shape[0], expert_down.shape[1]
-    kv = w_keyval.shape[1] // 2
-    chunks = kv // LANES
     y, hidden, moe, queries, keyval, mixture, grad_gu, grad_dn = forward_call(
         count, tokens, lengths, routes, attn_gain, w_query, w_keyval, w_out, ffn_gain, w_router,
         expert_gate_up, expert_down, cotangent,
     )
-    cos, sin = rope_constants(seq_len)
-    cos = lax.dynamic_slice_in_dim(jnp.asarray(cos), z * rows, rows, 0)
-    sin = lax.dynamic_slice_in_dim(jnp.asarray(sin), z * rows, rows, 0)
-    local_pos = z * rows + jnp.arange(rows, dtype=jnp.int32)
-    all_pos = jnp.arange(seq_len, dtype=jnp.int32)
-    low = jnp.arange(LANES) < HEAD_DIM
-    roll = lambda v: jnp.roll(v, HEAD_DIM, -1)
-    sums = [0.0] * 6
-    input_grads = []
-    for m in range(micros):
-        length = lengths[m, 0]
-        live = (local_pos < length)[:, None]
-        x_rows = tokens[m, 0].astype(F32)
-        scale_one = rms_scale(x_rows)
-        normed = (x_rows * scale_one * attn_gain).astype(BF)
-        scale_two = rms_scale(hidden[m])
-        normed2 = (hidden[m] * scale_two * ffn_gain).astype(BF)
-        logits = nn(normed2, w_router)
-        ids = lax.dynamic_slice_in_dim(routes[m, 0], z * rows, rows, 0)
-        named = (ids[:, :, None] == jnp.arange(experts)).any(1) & live
-        masked = jnp.where(named, logits, NEG_FILL)
-        raised = jnp.where(named, jnp.exp(masked - masked.max(-1, keepdims=True)), 0.0)
-        total = raised.sum(-1, keepdims=True)
-        gate = raised / jnp.where(total > 0, total, 1.0)
-        d_gate = moe[m, :, model : model + experts]
-        d_logits = (gate * (d_gate - jnp.sum(gate * d_gate, -1, keepdims=True))).astype(BF)
-        d_normed2 = moe[m, :, :model] + nt(d_logits, w_router)
-        part, gain_two = norm_backward(d_normed2, hidden[m], scale_two, ffn_gain)
-        d_hidden = cotangent[m, 0].astype(F32) + part
-        d_attn = jnp.where(live, d_hidden, 0.0).astype(BF)
-        d_mix = nt(d_attn, w_out).astype(BF)
-        d_query, d_key, d_value = [], [], []
-        for i in range(chunks):
-            lanes = slice(i * LANES, (i + 1) * LANES)
-            key, value = keyval[m, :, lanes], keyval[m, :, kv + i * LANES : kv + (i + 1) * LANES]
-            first, second = (
-                d_mix[:, c * LANES : (c + 1) * LANES] for c in (2 * i, 2 * i + 1)
-            )
-            d_stack = jnp.concatenate(
-                [
-                    jnp.where(low, first, 0), jnp.where(low, roll(first), 0),
-                    jnp.where(low, 0, roll(second)), jnp.where(low, 0, second),
-                ]
-            ).astype(BF)
-            s = nt(queries[m, i], key) * ATTENTION_SCALE
-            ok = (all_pos[None, :] <= jnp.tile(local_pos, 4)[:, None]) & (all_pos < length)[None, :]
-            prob = jax.nn.softmax(jnp.where(ok, s, NEG_FILL), axis=-1)
-            d_prob = nt(d_stack, value)
-            d_scores = (prob * (d_prob - jnp.sum(prob * d_prob, -1, keepdims=True))).astype(BF)
-            dq = nn(d_scores, key) * ATTENTION_SCALE
-            d_key.append(tn(d_scores, queries[m, i]) * ATTENTION_SCALE)
-            d_value.append(tn(prob.astype(BF), d_stack))
-            q = [dq[k * rows : (k + 1) * rows] for k in range(4)]
-            d_query += [jnp.where(low, q[0], roll(q[1])), jnp.where(low, roll(q[2]), q[3])]
-        d_query = plain_rope(jnp.concatenate(d_query, 1), cos, -sin).astype(BF)
-        d_kv = lax.psum_scatter(
-            jnp.concatenate(d_key + d_value, 1).astype(BF), "expert", scatter_dimension=0, tiled=True
-        ).astype(F32)
-        d_kv = jnp.concatenate([plain_rope(d_kv[:, :kv], cos, -sin), d_kv[:, kv:]], 1).astype(BF)
-        d_normed = nt(d_query, w_query) + nt(d_kv, w_keyval)
-        part, gain_one = norm_backward(d_normed, x_rows, scale_one, attn_gain)
-        input_grads.append(d_hidden + part)
-        terms = (
-            gain_one, tn(normed, d_query), tn(normed, d_kv), tn(mixture[m], d_attn), gain_two,
-            tn(normed2, d_logits),
-        )
-        sums = [a + b for a, b in zip(sums, terms)]
-    both = ("dp", "expert")
-    scatter = lambda v: lax.psum_scatter(v, both, scatter_dimension=0, tiled=True)
-    dense = [
-        scatter(v if k in (0, 4, 5) else v.astype(BF)).astype(F32) for k, v in enumerate(sums)
-    ]
-    spread = lambda v: lax.psum_scatter(v, "dp", scatter_dimension=1, tiled=True).astype(F32)
+    input_grad, gu, dn, dense, small = backward_call(
+        count, devices, tokens, lengths, routes, attn_gain, w_query, w_keyval, w_out, ffn_gain,
+        w_router, cotangent, local, ff, hidden, moe, queries, keyval, mixture, grad_gu, grad_dn,
+    )
+    block = model // devices // count
+    if dense.shape[1] != block:
+        first = lax.rem(lax.axis_index("expert") * block, dense.shape[1])
+        dense = lax.dynamic_slice_in_dim(dense, first, block, 1)
+        small = lax.dynamic_slice_in_dim(small, first, block, 0)
     return (
-        y, jnp.stack(input_grads)[:, None], *dense, spread(grad_gu),
-        spread(grad_dn.reshape(local, ff, model)),
+        y, input_grad, small[:, experts], dense[0], dense[1], dense[2], small[:, experts + 1],
+        small[:, :experts], gu, dn,
     )
 
 

time: 1050 us -> 428 us (0.41)
  waiting for transfers between devices: 601 us -> 0 us
  Pallas kernels: 243 us -> 408 us
  matrix products: 77 us -> 0 us
  blocking collectives: 37.3 us -> 0 us
  other arithmetic: 32.8 us -> 0 us
  local copies, waits for them, and re-layouts: 34.3 us -> 15.4 us
  between operations: 15.8 us -> 0.95 us
    reduce_scatter x7 -> x0, waiting for transfers between devices: 488 us -> none  [the longest x3 364 us: on_device(): lax.psum_scatter(v, both, scatter_dimension=0, tiled=True)]
    pallas_call x0 -> x1, Pallas kernels: none -> 165 us  [backward_call(): pl.pallas_call(functools.partial(backward_kernel, dims, plane), out_shape...]
    unnamed x9 -> x0, waiting for transfers between devices: 113 us -> none
    dot_general x58 -> x0, matrix products: 77 us -> none  [dot_of(): lax.dot_general(left, right, (((left_dim,), (right_dim,)), ((), ())), pre...]
    unnamed x1 -> x0, blocking collectives: 37.3 us -> none
    convert_element_type x16 -> x0, other arithmetic: 14.8 us -> none  [the longest x2 4.91 us: on_device(): lax.psum_scatter(v, 'dp', scatter_dimension=1, tiled=True).astype(F32)]
  transfers between devices with their start and end apart: 8 -> 0, of which waited for: 6 -> 0; matrix products, arithmetic and copies ran while one was open for 9% -> 0% of each run, Pallas kernels for 0% -> 0%
where the time goes in v2:
time: 428 us; the launch traced here: 424 us
  Pallas kernels  408 us (95%)
  local copies, waits for them, and re-layouts  15.4 us (4%)
    pallas_call x1, Pallas kernels, forward_call(): pl.pallas_call(functools.partial(forward_kernel, dims), out_shape=out_sha...  243 us
    pallas_call x1, Pallas kernels, backward_call(): pl.pallas_call(functools.partial(backward_kernel, dims, plane), out_shape...  165 us
    unnamed x14, local copies, waits for them, and re-layouts  12.1 us

profile of v2, /device:TPU:0, one launch (start us, length us, event | category | flops | bytes accessed | tf_op | source)
XLA Modules:
  0.0 424.2 jit_solution(1010045709556678430)
XLA Ops:
  0.6 1.3 copy.33.lengths
  1.9 1.6 copy.35.router
  3.5 1.8 copy.34.routes
  5.3 242.8 %layer_forward.1 = (bf16[2,1,128,1024]{3,2,1,0:T(8,128)(2,1)}, f32[2,128,1024]{2,1,0:T(8,128)}, f32[2,128,1152]{2,1,0:T(8,128)}, bf16[2,4,512,128]{3,2,1,0:T(8,1...) custom-call(s32[2,1]{1,0:T(2,128)} %copy.33.lengths, ...), custom_call_target="tpu_custom_call" | custom-call | tf_op jit(solution)/shard_map/layer_forward/pallas_call | solution.py:695
  248.1 0.0 copy-start.2
  248.1 165.0 %layer_backward.1 = (f32[2,1,128,1024]{3,2,1,0:T(8,128)}, f32[4,128,1024]{2,1,0:T(8,128)}, f32[4,64,1024]{2,1,0:T(8,128)}, f32[3,32,1024]{2,1,0:T(8,128)}, f32[32,128]{1,0:T(8,128)}) custom-call(s32[2,1]{1,0:T(2,128)} %copy.33.lengths, bf16[2,1,128,1024]{3,2,1,0:T(8,128)(2,1)} %tokens.3, bf16[2,1,128,1024]{3,2,1,0:T(8,128)(2,1)} %cot.3, ...), custom_call_target="tpu_custom_call" | custom-call | tf_op jit(solution)/shard_map/layer_backward/pallas_call | solution.py:1261
  413.1 0.0 copy-start
  413.1 1.6 slice_reduce_fusion
  414.7 1.4 copy.39
  416.1 1.8 slice_bitcast_fusion
  417.9 0.0 copy-done.2
  417.9 0.8 copy.44
  418.7 2.3 copy.45
  421.0 0.0 copy-done
  421.0 0.0 copy-start.1
  421.0 1.3 copy.46
  422.3 0.6 copy-done.1
  422.9 1.0 copy.47
Async XLA Ops:
  248.1 169.8 %copy-start.2 = (bf16[2,1,128,1024]{3,2,1,0:T(8,128)(2,1)S(1)}, bf16[2,1,128,1024]{3,2,1,0:T(8,128)(2,1)}, u32[]{:S(2)}) copy-start(bf16[2,1,128,1024]{3,2,1,0:T(8,128)(2,1)} %get-tuple-element.71) | copy-start | bytes 1572868
  413.1 7.9 %copy-start = (f32[4,128,1024]{2,1,0:T(8,128)S(1)}, f32[4,128,1024]{2,1,0:T(8,128)}, u32[]{:S(2)}) copy-start(f32[4,128,1024]{2,1,0:T(8,128)} %get-tuple-element.79) | copy-start | bytes 6291460
  421.0 2.0 copy-start.1
